TPU v7x, 32 devices: a whole 2x2x4 slice. The times are simulated.
32 devices in a mesh: gx: 8 (over z, y), gy: 4 (over x, core).
Axes of the slice: x: 2, y: 2, z: 4, core: 2. Of those that a mesh axis runs over, the one named last changes fastest.
Arguments:
- fields: float32 [5, 64, 128, 512], P(None, None, 'gx', 'gy'), may hold values from -6 to 6
- previous: float32 [5, 64, 128, 512], P(None, None, 'gx', 'gy'), may hold values from -6 to 6
- heights: int32 [128, 512], P('gx', 'gy'), may hold values from 0 to 32, as said below
- part_cells: int32 [8, 4, 9216], P('gx', 'gy'), may hold values from 0 to 131071, as said below
- part_offsets: float32 [3, 8, 4, 9216], P(None, 'gx', 'gy'), may hold values from 0 to 1
- cross_counts: int32 [8, 4, 2], P('gx', 'gy'), may hold values from 0 to 512, as said below
Outputs:
- updated: float32 [5, 64, 128, 512], P(None, None, 'gx', 'gy')
- accumulated: float32 [5, 64, 128, 512], P(None, None, 'gx', 'gy')
- part_moved: float32 [3, 8, 4, 9216], P(None, 'gx', 'gy')
Inputs may be any that keep to these rules, and one draw needn't show every extreme that they name: `heights`: 0 for open ground; some column reaches 32. `part_cells`: the slots 8192 to 8703 lie in the last along-wind cell plane of their device, the slots from 8704 on in the first; slots 8192 and 8704 lie in the last cross-wind column. `cross_counts`: some device has 512 downwind crossers.
All inputs are finite; a program needn't handle non-finite values. Where the computation divides by a largest or mean magnitude, that divisor is 1e-20 or more.
Results may differ from a plain program's by a relative error of at most 0.00007.
Values sent between devices are 32-bit elements; how exact they have to be, the bound alone decides.
A program may use at most 128 MiB of HBM per device.

v0:
```python
import math

import jax
import jax.numpy as jnp
from jax import lax
from jax.sharding import PartitionSpec as P

P_KEEP = 8192
CAP = 512


courant = 0.9
viscosity = 0.1
prior_weight = -5.0 / 9.0
section_weight = 15.0 / 16.0


def padded_2(array, sides, width, wrap):
    for axis, dim in sides:
        peers, length = (lax.axis_size(axis), array.shape[dim])
        up = [(i, (i + 1) % peers) for i in range(peers if wrap else peers - 1)]
        down = [(j, i) for i, j in up]
        last = lax.slice_in_dim(array, length - width, length, axis=dim)
        initial = lax.slice_in_dim(array, 0, width, axis=dim)
        before = lax.ppermute(last, axis, up)
        after = lax.ppermute(initial, axis, down)
        array = jnp.concatenate([before, array, after], axis=dim)
    return array


def from_behind(value, axis, steps):
    count = lax.axis_size(axis)
    pairs = [(source, (source + steps) % count) for source in range(count)]
    return lax.ppermute(value, axis, pairs)


def fluid_cells(heights, levels):
    level_ids = lax.broadcasted_iota(jnp.int32, (levels,) + heights.shape, 0)
    return (level_ids >= heights[None]).astype(jnp.float32)


def advance_field(padded, velocity, fluid, time_step, prior):
    width_x = padded.shape[1] - 4
    width_y = padded.shape[2] - 4

    def along(offset):
        return padded[:, 2 + offset : 2 + offset + width_x, 2 : 2 + width_y]

    def across(offset):
        return padded[:, 2 : 2 + width_x, 2 + offset : 2 + offset + width_y]

    center = along(0)
    grad_x = (8.0 * (along(1) - along(-1)) - (along(2) - along(-2))) / 12.0
    grad_y = (8.0 * (across(1) - across(-1)) - (across(2) - across(-2))) / 12.0
    stacked = jnp.pad(center, ((1, 1), (0, 0), (0, 0)))
    level_up = stacked[2:]
    level_down = stacked[:-2]
    grad_z = 0.5 * (level_up - level_down)
    laplace = along(1) + along(-1) + across(1) + across(-1) + level_up + level_down - 6.0 * center
    tendency = viscosity * laplace - (
        velocity[0] * grad_x + velocity[1] * grad_y + velocity[2] * grad_z
    )
    accumulated = prior_weight * prior + tendency
    updated = center + section_weight * time_step * accumulated
    return (updated * fluid, accumulated * fluid)


def sample_dense(vel_table, level_ids, row_index, col_index, rows_len, cols_len, offsets):
    total = level_ids.shape[0]
    block = math.gcd(total, 1024)
    blocks = total // block
    table_rows = vel_table.shape[0]
    row_key = (level_ids * rows_len + row_index).reshape(blocks, block)
    col_key = col_index.reshape(blocks, block)
    frac_x = offsets[0].reshape(blocks, block)
    frac_y = offsets[1].reshape(blocks, block)

    def one_block(pieces):
        keys, cols, along_frac, across_frac = pieces
        targets = lax.broadcasted_iota(jnp.int32, (block, table_rows), 1)
        row_weight = jnp.where(
            targets == keys[:, None], 1.0 - along_frac[:, None], 0.0
        ) + jnp.where(targets == keys[:, None] + 1, along_frac[:, None], 0.0)
        picked = jnp.dot(
            row_weight,
            vel_table,
            precision=lax.Precision.HIGHEST,
            preferred_element_type=jnp.float32,
        ).reshape(block, 3, cols_len)
        col_ids = lax.broadcasted_iota(jnp.int32, (block, cols_len), 1)
        col_weight = jnp.where(
            col_ids == cols[:, None], 1.0 - across_frac[:, None], 0.0
        ) + jnp.where(col_ids == cols[:, None] + 1, across_frac[:, None], 0.0)
        return jnp.sum(picked * col_weight[:, None, :], axis=2)

    result = lax.map(one_block, (row_key, col_key, frac_x, frac_y))
    return result.reshape(total, 3).T


def local(fields, previous, heights, part_cells, part_offsets, cross_counts):
    levels = fields.shape[1]
    width_x = fields.shape[2]
    width_y = fields.shape[3]
    extended = padded_2(fields, (("gx", 2),), 2, True)
    padded = padded_2(extended, (("gy", 3),), 2, False)
    speeds = jnp.max(jnp.abs(fields[0]) + jnp.abs(fields[1]) + jnp.abs(fields[2]))
    fastest = lax.pmax(speeds, ("gx", "gy"))
    time_step = courant / (fastest + 1e-06)
    fluid = fluid_cells(heights, levels)
    velocity = fields[0:3]
    new_list = []
    acc_list = []
    for field_id in range(fields.shape[0]):
        new_one, acc_one = advance_field(
            padded[field_id], velocity, fluid, time_step, previous[field_id]
        )
        new_list.append(new_one)
        acc_list.append(acc_one)
    updated = jnp.stack(new_list)
    accumulated = jnp.stack(acc_list)
    rows_len = width_x + 4
    cols_len = width_y + 4
    vel_table = jnp.transpose(padded[0:3], (1, 2, 0, 3)).reshape(levels * rows_len, 3 * cols_len)
    local_cells = part_cells[0, 0]
    offsets = part_offsets[:, 0, 0]
    counts = cross_counts[0, 0]
    level_ids = local_cells // (width_x * width_y)
    col_local = local_cells % width_y
    block_index = lax.broadcasted_iota(jnp.int32, (CAP,), 0)
    live_right = (block_index < counts[0]).astype(jnp.float32)
    live_left = (block_index < counts[1]).astype(jnp.float32)
    row_index = local_cells // width_y % width_x + 2
    part_vel = sample_dense(
        vel_table, level_ids, row_index, col_local + 2, rows_len, cols_len, offsets
    )
    advanced = offsets + time_step * part_vel
    right_block = advanced[:, P_KEEP : P_KEEP + CAP] * live_right
    left_block = advanced[:, P_KEEP + CAP :] * live_left
    from_left = from_behind(right_block, "gx", 1)
    from_right = from_behind(left_block, "gx", -1)
    resident = advanced[:, :P_KEEP]
    part_moved = jnp.concatenate([resident, from_left, from_right], axis=-1)
    return (updated, accumulated, part_moved.reshape(3, 1, 1, -1))


def solution(mesh):
    placed = (
        P(None, None, "gx", "gy"),
        P(None, None, "gx", "gy"),
        P("gx", "gy"),
        P("gx", "gy", None),
        P(None, "gx", "gy", None),
        P("gx", "gy", None),
    )
    return jax.shard_map(
        local,
        mesh=mesh,
        in_specs=placed,
        out_specs=(P(None, None, "gx", "gy"), P(None, None, "gx", "gy"), P(None, "gx", "gy", None)),
        check_vma=False,
    )
```

profile of v0, /device:TPU:0, one launch (start us, length us, event | category | flops | bytes accessed | tf_op | source)
XLA Modules:
  0.0 287.1 jit_solution(5219706136864873485)
XLA Ops:
  0.7 2.0 fusion.76
  2.7 6.1 %collective-permute-start.1 = (f32[5,64,2,128]{3,1,2,0:T(8,128)S(1)}, f32[5,64,2,128]{3,1,2,0:T(8,128)}, u32[]{:S(2)}, u32[]{:S(2)}) collective-permute-start(f32[5,64,2,128]{3,1,2,0:T(8,128)S(1)} %copy.49), channel_id=1, source_target_pairs={{4,0},{8,4},{12,8},{16,12},{20,16},{24,20},{28,24},{0,28},{5,1},{9... | collective-permute-start | bytes 983048 | tf_op jit(solution)/shard_map/ppermute | solution.py:26
  9.5 5.1 %copy.32 = f32[5,64,16,128]{1,3,2,0:T(8,128)} copy(f32[5,64,16,128]{3,2,1,0:T(8,128)} %param.8) | data formatting | bytes 5242880 | tf_op args[0]
  16.8 2.8 add_reduce_fusion
  25.3 2.1 collective-permute-start.2
  30.0 42.4 %pmax.7 = f32[]{:T(128)} all-reduce(f32[]{:T(128)} %add_reduce_fusion), channel_id=1, replica_groups=mesh['gx'=8,'gy'=4] {'gx','gy'}, use_global_device_ids=true, to_apply=%region_1.0 | all-reduce | flops 1 | bytes 8 | tf_op jit(solution)/shard_map/pmax | solution.py:107
  72.4 2.4 copy.54
  74.8 2.4 copy.53
  81.9 5.5 %pad_maximum_fusion = f32[5,64,20,132]{1,3,2,0:T(8,128)S(1)} fusion(f32[5,64,20,2]{1,3,2,0:T(2,128)} %collective-permute-done.3, f32[5,64,2,128]{1,3,2,0:T(8,128)S(1)} %copy.33, f32[5,64,16,128]{1,3,2,0:T(8,128)} %copy.32, f32[5,64,2,128]{1,3,2,0:T(8,128)S(1)} %copy.31, f32[5,64,20,2]{1,3,2,0:T(2,128)} %collective-permute-done.2), kind=kLoop, calls=%fused_computation.25 | loop fusion | flops 3379200 | bytes 6758400 | tf_op jit(solution)/shard_map/concatenate | solution.py:27
  87.4 2.3 slice_bitcast_fusion
  96.5 7.6 %copy.42 = f32[64,20,3,132]{3,2,1,0:T(4,128)} copy(f32[64,20,3,132]{0,3,1,2:T(8,128)} %slice_bitcast_fusion) | data formatting | bytes 4055040 | tf_op jit(solution)/shard_map/transpose | solution.py:123
  104.1 7.0 %reshape.144 = f32[1280,396]{1,0:T(8,128)} reshape(f32[64,20,3,132]{3,2,1,0:T(4,128)} %copy.42) | data formatting | bytes 4055040 | tf_op jit(solution)/shard_map/reshape | solution.py:123
  111.1 137.9 %while.10 = (s32[]{:T(128)}, f32[9,1024,3]{1,2,0:T(4,128)S(1)}, s32[9,1024]{1,0:T(8,128)}, f32[9,1024]{1,0:T(8,128)S(1)}, f32[1280,396]{1,0:T(8,128)}, /*index=5...) while((s32[]{:T(128)}, f32[9,1024,3]{1,2,0:T(4,128)S(1)}, s32[9,1024]{1,0:T(8,128)}, ...), condition=%wide.region_4.5_spmd, body=%wide.region_2.4_spmd.sunk | while | flops 6236582912 | bytes 9740393 | solution.py:96
  112.9 10.8 %fusion.84 = f32[1024,396]{0,1:T(8,128)} fusion(f32[1280,396]{1,0:T(8,128)} %get-tuple-element.174, f32[1024]{0:T(1024)S(1)} %bitcast.142, s32[1024]{0:T(1024)S(1)} %broadcast_add_fusion.4, f32[1024]{0:T(1024)S(1)} %broadcast_subtract_fusion.4, s32[1024]{0:T(1024)S(1)} %bitcast.144), kind=kOutput, calls=%fused_computation.clone.1 | convolution fusion | flops 6235095040 | bytes 3665920 | tf_op jit(solution)/shard_map/while/body/eval_jaxpr/dot_general | solution.py:84
  128.2 10.8 %fusion.84 = f32[1024,396]{0,1:T(8,128)} fusion(f32[1280,396]{1,0:T(8,128)} %get-tuple-element.174, f32[1024]{0:T(1024)S(1)} %bitcast.142, s32[1024]{0:T(1024)S(1)} %broadcast_add_fusion.4, f32[1024]{0:T(1024)S(1)} %broadcast_subtract_fusion.4, s32[1024]{0:T(1024)S(1)} %bitcast.144), kind=kOutput, calls=%fused_computation.clone.1 | convolution fusion | flops 6235095040 | bytes 3665920 | tf_op jit(solution)/shard_map/while/body/eval_jaxpr/dot_general | solution.py:84
  143.6 10.8 %fusion.84 = f32[1024,396]{0,1:T(8,128)} fusion(f32[1280,396]{1,0:T(8,128)} %get-tuple-element.174, f32[1024]{0:T(1024)S(1)} %bitcast.142, s32[1024]{0:T(1024)S(1)} %broadcast_add_fusion.4, f32[1024]{0:T(1024)S(1)} %broadcast_subtract_fusion.4, s32[1024]{0:T(1024)S(1)} %bitcast.144), kind=kOutput, calls=%fused_computation.clone.1 | convolution fusion | flops 6235095040 | bytes 3665920 | tf_op jit(solution)/shard_map/while/body/eval_jaxpr/dot_general | solution.py:84
  158.9 10.8 %fusion.84 = f32[1024,396]{0,1:T(8,128)} fusion(f32[1280,396]{1,0:T(8,128)} %get-tuple-element.174, f32[1024]{0:T(1024)S(1)} %bitcast.142, s32[1024]{0:T(1024)S(1)} %broadcast_add_fusion.4, f32[1024]{0:T(1024)S(1)} %broadcast_subtract_fusion.4, s32[1024]{0:T(1024)S(1)} %bitcast.144), kind=kOutput, calls=%fused_computation.clone.1 | convolution fusion | flops 6235095040 | bytes 3665920 | tf_op jit(solution)/shard_map/while/body/eval_jaxpr/dot_general | solution.py:84
  174.2 10.8 %fusion.84 = f32[1024,396]{0,1:T(8,128)} fusion(f32[1280,396]{1,0:T(8,128)} %get-tuple-element.174, f32[1024]{0:T(1024)S(1)} %bitcast.142, s32[1024]{0:T(1024)S(1)} %broadcast_add_fusion.4, f32[1024]{0:T(1024)S(1)} %broadcast_subtract_fusion.4, s32[1024]{0:T(1024)S(1)} %bitcast.144), kind=kOutput, calls=%fused_computation.clone.1 | convolution fusion | flops 6235095040 | bytes 3665920 | tf_op jit(solution)/shard_map/while/body/eval_jaxpr/dot_general | solution.py:84
  189.5 10.8 %fusion.84 = f32[1024,396]{0,1:T(8,128)} fusion(f32[1280,396]{1,0:T(8,128)} %get-tuple-element.174, f32[1024]{0:T(1024)S(1)} %bitcast.142, s32[1024]{0:T(1024)S(1)} %broadcast_add_fusion.4, f32[1024]{0:T(1024)S(1)} %broadcast_subtract_fusion.4, s32[1024]{0:T(1024)S(1)} %bitcast.144), kind=kOutput, calls=%fused_computation.clone.1 | convolution fusion | flops 6235095040 | bytes 3665920 | tf_op jit(solution)/shard_map/while/body/eval_jaxpr/dot_general | solution.py:84
  204.9 10.8 %fusion.84 = f32[1024,396]{0,1:T(8,128)} fusion(f32[1280,396]{1,0:T(8,128)} %get-tuple-element.174, f32[1024]{0:T(1024)S(1)} %bitcast.142, s32[1024]{0:T(1024)S(1)} %broadcast_add_fusion.4, f32[1024]{0:T(1024)S(1)} %broadcast_subtract_fusion.4, s32[1024]{0:T(1024)S(1)} %bitcast.144), kind=kOutput, calls=%fused_computation.clone.1 | convolution fusion | flops 6235095040 | bytes 3665920 | tf_op jit(solution)/shard_map/while/body/eval_jaxpr/dot_general | solution.py:84
  220.2 10.8 %fusion.84 = f32[1024,396]{0,1:T(8,128)} fusion(f32[1280,396]{1,0:T(8,128)} %get-tuple-element.174, f32[1024]{0:T(1024)S(1)} %bitcast.142, s32[1024]{0:T(1024)S(1)} %broadcast_add_fusion.4, f32[1024]{0:T(1024)S(1)} %broadcast_subtract_fusion.4, s32[1024]{0:T(1024)S(1)} %bitcast.144), kind=kOutput, calls=%fused_computation.clone.1 | convolution fusion | flops 6235095040 | bytes 3665920 | tf_op jit(solution)/shard_map/while/body/eval_jaxpr/dot_general | solution.py:84
  235.5 10.8 %fusion.84 = f32[1024,396]{0,1:T(8,128)} fusion(f32[1280,396]{1,0:T(8,128)} %get-tuple-element.174, f32[1024]{0:T(1024)S(1)} %bitcast.142, s32[1024]{0:T(1024)S(1)} %broadcast_add_fusion.4, f32[1024]{0:T(1024)S(1)} %broadcast_subtract_fusion.4, s32[1024]{0:T(1024)S(1)} %bitcast.144), kind=kOutput, calls=%fused_computation.clone.1 | convolution fusion | flops 6235095040 | bytes 3665920 | tf_op jit(solution)/shard_map/while/body/eval_jaxpr/dot_general | solution.py:84
  249.2 2.6 collective-permute-start.4
  251.8 2.3 collective-permute-start.5
  254.1 8.2 %bitcast_dynamic-update-slice_fusion.5 = (f32[5,64,16,128]{1,3,2,0:T(8,128)S(1)}, f32[64,16,128]{0,2,1:T(8,128)S(1)}) fusion(s32[16,128]{1,0:T(8,128)S(1)} %copy-done.21, f32[5,64,16,128]{1,3,2,0:T(8,128)} %copy.32, f32[64,20,132]{0,2,1:T(8,128)} %copy-done.6, f32[64,16,128]{0,2,1:T(8,128)} %slice.364, f32[1,64,16,128]{1,3,2,0:T(8,128)} %copy.50), kind=kLoop, calls=%fused_computation.99 | loop fusion | flops 3932159 | bytes 8921088
  262.3 2.0 bitcast_dynamic-update-slice_fusion.4
  264.4 2.0 bitcast_dynamic-update-slice_fusion.3
  266.5 2.0 bitcast_dynamic-update-slice_fusion.2
  268.5 2.3 bitcast_dynamic-update-slice_fusion.1
  273.2 2.3 copy-done.8
  275.5 5.4 %copy.45 = f32[5,64,16,128]{3,2,1,0:T(8,128)} copy(f32[5,64,16,128]{1,3,2,0:T(8,128)} %copy-done.9) | data formatting | bytes 5242880
  280.9 5.4 %copy.44 = f32[5,64,16,128]{3,2,1,0:T(8,128)} copy(f32[5,64,16,128]{1,3,2,0:T(8,128)} %copy-done.8) | data formatting | bytes 5242880
  (192 shorter events, 65.6 us)
Async XLA Ops:
  0.6 14.5 %copy-start.25 = (s32[1,1,9216]{2,1,0:T(1,128)S(1)}, s32[1,1,9216]{2,1,0:T(1,128)}, u32[]{:S(2)}) copy-start(s32[1,1,9216]{2,1,0:T(1,128)} %param.11) | copy-start | bytes 110596
  0.6 16.0 %copy-start.23 = (f32[3,1,1,9216]{3,2,1,0:T(1,128)S(1)}, f32[3,1,1,9216]{3,2,1,0:T(1,128)}, u32[]{:S(2)}) copy-start(f32[3,1,1,9216]{3,2,1,0:T(1,128)} %param.12) | copy-start | bytes 331780
  2.7 18.9 %collective-permute-start.1 = (f32[5,64,2,128]{3,1,2,0:T(8,128)S(1)}, f32[5,64,2,128]{3,1,2,0:T(8,128)}, u32[]{:S(2)}, u32[]{:S(2)}) collective-permute-start(f32[5,64,2,128]{3,1,2,0:T(8,128)S(1)} %copy.49), channel_id=1, source_target_pairs={{4,0},{8,4},{12,8},{16,12},{20,16},{24,20},{28,24},{0,28},{5,1},{9... | collective-permute-start | bytes 983048 | tf_op jit(solution)/shard_map/ppermute | solution.py:26
  9.5 10.1 %copy-start.26 = (s32[1,1,2]{2,1,0:T(1,128)S(1)}, s32[1,1,2]{2,1,0:T(1,128)}, u32[]{:S(2)}) copy-start(s32[1,1,2]{2,1,0:T(1,128)} %param.13) | copy-start | bytes 28
  9.5 10.7 %copy-start.18 = (f32[5,64,16,128]{3,2,1,0:T(8,128)S(1)}, f32[5,64,16,128]{3,2,1,0:T(8,128)}, u32[]{:S(2)}) copy-start(f32[5,64,16,128]{3,2,1,0:T(8,128)} %param.9) | copy-start | bytes 7864324
  9.5 13.3 %collective-permute-start = (f32[5,64,2,128]{3,1,2,0:T(8,128)}, f32[5,64,2,128]{3,1,2,0:T(8,128)}, u32[]{:S(2)}, u32[]{:S(2)}) collective-permute-start(f32[5,64,2,128]{3,1,2,0:T(8,128)} %copy.48), channel_id=1, source_target_pairs={{0,4},{4,8},{8,12},{12,16},{16,20},{20,24},{24,28},{28,0},{1,5},{5... | collective-permute-start | bytes 983048 | tf_op jit(solution)/shard_map/ppermute | solution.py:25
  24.0 53.1 %copy-start.20 = (f32[1,64,16,128]{3,2,1,0:T(8,128)S(1)}, f32[1,64,16,128]{3,2,1,0:T(8,128)}, u32[]{:S(2)}) copy-start(f32[1,64,16,128]{3,2,1,0:T(8,128)} %get-tuple-element.89) | copy-start | bytes 1572868
  24.0 54.5 %copy-start.19 = (f32[1,64,16,128]{3,2,1,0:T(8,128)S(1)}, f32[1,64,16,128]{3,2,1,0:T(8,128)}, u32[]{:S(2)}) copy-start(f32[1,64,16,128]{3,2,1,0:T(8,128)} %get-tuple-element.90) | copy-start | bytes 1572868
  25.3 56.5 %collective-permute-start.2 = (f32[5,64,20,2]{1,3,2,0:T(2,128)S(1)}, f32[5,64,20,2]{1,3,2,0:T(2,128)}, u32[]{:S(2)}, u32[]{:S(2)}) collective-permute-start(f32[5,64,20,2]{1,3,2,0:T(2,128)S(1)} %get-tuple-element.85), channel_id=1, source_target_pairs={{0,1},{1,2},{2,3},{4,5},{5,6},{6,7},{8,9},{9,10},{10,11},{12,13},{... | collective-permute-start | bytes 153608 | tf_op jit(solution)/shard_map/ppermute | solution.py:25
  27.4 54.4 %collective-permute-start.3 = (f32[5,64,20,2]{1,3,2,0:T(2,128)S(1)}, f32[5,64,20,2]{1,3,2,0:T(2,128)}, u32[]{:S(2)}, u32[]{:S(2)}) collective-permute-start(f32[5,64,20,2]{1,3,2,0:T(2,128)S(1)} %get-tuple-element.86), channel_id=1, source_target_pairs={{1,0},{2,1},{3,2},{5,4},{6,5},{7,6},{9,8},{10,9},{11,10},{13,12},{... | collective-permute-start | bytes 153608 | tf_op jit(solution)/shard_map/ppermute | solution.py:26
  90.2 3.1 %copy-start.2 = (f32[64,20,132]{0,2,1:T(8,128)}, f32[64,20,132]{0,2,1:T(8,128)S(1)}, u32[]{:S(2)}) copy-start(f32[64,20,132]{0,2,1:T(8,128)S(1)} %get-tuple-element.82) | copy-start | bytes 2027524
  90.2 4.1 %copy-start.4 = (f32[64,20,132]{0,2,1:T(8,128)}, f32[64,20,132]{0,2,1:T(8,128)S(1)}, u32[]{:S(2)}) copy-start(f32[64,20,132]{0,2,1:T(8,128)S(1)} %get-tuple-element.83) | copy-start | bytes 2027524
  90.2 5.3 %copy-start.6 = (f32[64,20,132]{0,2,1:T(8,128)}, f32[64,20,132]{0,2,1:T(8,128)S(1)}, u32[]{:S(2)}) copy-start(f32[64,20,132]{0,2,1:T(8,128)S(1)} %get-tuple-element.84) | copy-start | bytes 2027524
  111.1 138.0 %copy-start.24 = (f32[3,1,1,9216]{3,2,1,0:T(1,128)S(1)}, f32[3,1,1,9216]{3,2,1,0:T(1,128)}, u32[]{:S(2)}) copy-start(f32[3,1,1,9216]{3,2,1,0:T(1,128)} %param.12) | copy-start | bytes 331780
  111.1 142.9 %copy-start.21 = (s32[16,128]{1,0:T(8,128)S(1)}, s32[16,128]{1,0:T(8,128)}, u32[]{:S(2)}) copy-start(s32[16,128]{1,0:T(8,128)} %param.10) | copy-start | bytes 24580
  249.2 23.5 %copy-start.22 = (f32[3,9216]{1,0:T(4,128)}, f32[3,9216]{1,0:T(4,128)S(1)}, u32[]{:S(2)}) copy-start(f32[3,9216]{1,0:T(4,128)S(1)} %bitcast_add_fusion) | copy-start | bytes 331780
  249.2 37.1 %collective-permute-start.4 = (f32[3,512]{1,0:T(4,128)S(1)}, f32[3,512]{1,0:T(4,128)S(1)}, u32[]{:S(2)}, u32[]{:S(2)}) collective-permute-start(f32[3,512]{1,0:T(4,128)S(1)} %get-tuple-element.94), channel_id=1, source_target_pairs={{0,4},{4,8},{8,12},{12,16},{16,20},{20,24},{24,28},{28,0},{1,5},{5... | collective-permute-start | bytes 18440 | tf_op jit(solution)/shard_map/ppermute | solution.py:34
  251.8 10.5 %slice-start = ((s8[5242880]{0:T(1024)(128)(4,1)}), s8[4194304]{0:T(1024)(128)(4,1)S(1)}, s32[]{:S(2)}) async-start(s8[5242880]{0:T(1024)(128)(4,1)} %bitcast.134), calls=%async_computation | async-start | bytes 8388608
  251.8 10.5 %slice-start.1 = ((s8[5242880]{0:T(1024)(128)(4,1)}), s8[1048576]{0:T(1024)(128)(4,1)S(1)}, s32[]{:S(2)}) async-start(s8[5242880]{0:T(1024)(128)(4,1)} %bitcast.134), calls=%async_computation.1 | async-start | bytes 2097152
  251.8 10.5 %copy-start.5 = (f32[64,20,132]{0,2,1:T(8,128)S(1)}, f32[64,20,132]{0,2,1:T(8,128)}, u32[]{:S(2)}) copy-start(f32[64,20,132]{0,2,1:T(8,128)} %copy-done.4) | copy-start | bytes 2027524
  251.8 10.5 %copy-start.13 = (f32[1,64,16,128]{1,3,2,0:T(8,128)S(1)}, f32[1,64,16,128]{1,3,2,0:T(8,128)}, u32[]{:S(2)}) copy-start(f32[1,64,16,128]{1,3,2,0:T(8,128)} %copy.51) | copy-start | bytes 1572868
  251.8 10.5 %copy-start.17 = (f32[64,16,128]{0,2,1:T(8,128)S(1)}, f32[64,16,128]{0,2,1:T(8,128)}, u32[]{:S(2)}) copy-start(f32[64,16,128]{0,2,1:T(8,128)} %slice.377) | copy-start | bytes 1572868
  251.8 34.5 %collective-permute-start.5 = (f32[3,512]{1,0:T(4,128)S(1)}, f32[3,512]{1,0:T(4,128)S(1)}, u32[]{:S(2)}, u32[]{:S(2)}) collective-permute-start(f32[3,512]{1,0:T(4,128)S(1)} %get-tuple-element.95), channel_id=1, source_target_pairs={{0,28},{4,0},{8,4},{12,8},{16,12},{20,16},{24,20},{28,24},{1,29},{... | collective-permute-start | bytes 18440 | tf_op jit(solution)/shard_map/ppermute | solution.py:34
  262.3 2.0 copy-start.3
  262.3 2.0 copy-start.12
  262.3 2.0 copy-start.16
  266.5 2.1 copy-start.7
  266.5 2.1 copy-start.10
  266.5 2.1 copy-start.14
  270.8 2.4 copy-start.9
  273.2 2.3 copy-start.8
  280.9 5.4 %slice-start.2 = ((f32[3,9216]{1,0:T(4,128)}), f32[3,8192]{1,0:T(4,128)S(1)}, s32[]{:S(2)}) async-start(f32[3,9216]{1,0:T(4,128)} %copy-done.22), calls=%async_computation.2 | async-start | bytes 262144 | tf_op jit(solution)/shard_map/slice | solution.py:141
  (4 other events, 7.6 us)
where the time goes:
time: 290 us; the launch traced here: 287 us
  matrix products  97.2 us (34%)
  local copies, waits for them, and re-layouts  80.1 us (28%)
  other arithmetic  50.7 us (17%)
  blocking collectives  42.4 us (15%)
  starting transfers between devices  14.3 us (5%)
    dot_general x9, matrix products, one_block(): jnp.dot(row_weight, vel_table, precision=lax.Precision.HIGHEST, preferred...  97.2 us
    pmax x1, blocking collectives, local(): fastest = lax.pmax(speeds, ('gx', 'gy'))  42.4 us
    unnamed x70, local copies, waits for them, and re-layouts  29.6 us
    unnamed x9, other arithmetic  16.3 us
    reshape x9, local copies, waits for them, and re-layouts, one_block(): picked = jnp.dot(row_weight, vel_table, precision=lax.Precision.HIGHEST,...  12.9 us
    reduce_sum x9, other arithmetic, one_block(): return jnp.sum(picked * col_weight[:, None, :], axis=2)  11.5 us
    transpose x2, local copies, waits for them, and re-layouts, local(): jnp.transpose(padded[0:3], (1, 2, 0, 3))  9.93 us
    add x9, other arithmetic, one_block(): jnp.where(col_ids == cols[:, None], 1.0 - across_frac[:, None], 0.0)  8.18 us
  transfers between devices with their start and end apart: 6, of which 0 were waited for; matrix products, arithmetic and copies ran while one was open for 19% of the time, Pallas kernels for 0%

commit v1 on v0

v1 whole, which is shorter than its diff:
```python
import functools

import jax
import jax.numpy as jnp
from jax import lax
from jax.experimental import pallas as pl
from jax.experimental.pallas import tpu as pltpu
from jax.sharding import PartitionSpec as P

P_KEEP = 8192
CAP = 512
LANES = 128
GROUP = 4
VMEM_BYTES = 50 * 2**20

courant = 0.9
viscosity = 0.1
prior_weight = -5.0 / 9.0
section_weight = 15.0 / 16.0

MESH = pl.DeviceIdType.MESH


def lane_ids(rows):
    return lax.broadcasted_iota(jnp.int32, (rows, LANES), 1)


def exchange_kernel(
    n_gx, n_gy, n_fields, levels, width_x,
    x_ref, low_ref, high_ref, corner_ref, cols_ref, speed_ref,
    planes, packed, from_left, from_right, speed_own, speed_row, speed_y, speed_x,
    send_sems, recv_sems, y_send, y_recv, x_send, x_recv,
):
    p = lax.axis_index("gx")
    q = lax.axis_index("gy")

    def at(dp, dq):
        return (lax.rem(p + dp + n_gx, n_gx), lax.rem(q + dq + n_gy, n_gy))

    barrier = pltpu.get_barrier_semaphore()
    peers = [at(d, 0) for d in range(1, n_gx)] + [at(0, d) for d in range(1, n_gy)]
    peers += [at(-1, -1), at(1, 1)]
    for peer in peers:
        pl.semaphore_signal(barrier, inc=1, device_id=peer, device_id_type=MESH)

    columns = n_fields * levels
    for slot, row in enumerate((0, 1, width_x - 2, width_x - 1)):
        planes[slot] = x_ref[pl.ds(row, columns, stride=width_x), :]
    pl.semaphore_wait(barrier, len(peers))

    def remote(src, dst, index, peer):
        return pltpu.make_async_remote_copy(
            src_ref=src, dst_ref=dst, send_sem=send_sems.at[index], recv_sem=recv_sems.at[index],
            device_id=peer, device_id_type=MESH,
        )

    copies = [
        remote(planes.at[pl.ds(0, 2)], high_ref, 0, at(-1, 0)),
        remote(planes.at[pl.ds(2, 2)], low_ref, 1, at(1, 0)),
        remote(planes.at[0, pl.ds(0, 3 * levels)], corner_ref, 2, at(-1, -1)),
    ]
    for copy in copies:
        copy.start()

    rows = levels * width_x

    def fastest_rows(i, best):
        start = pl.multiple_of(i * 64, 64)
        total = (
            jnp.abs(x_ref[pl.ds(start, 64), :])
            + jnp.abs(x_ref[pl.ds(rows + start, 64), :])
            + jnp.abs(x_ref[pl.ds(2 * rows + start, 64), :])
        )
        return jnp.maximum(best, jnp.max(total.reshape(8, 8, LANES), axis=0))

    speed_own[...] = lax.fori_loop(0, rows // 64, fastest_rows, jnp.zeros((8, LANES), jnp.float32))

    y_copies = []
    for d in range(1, n_gy):
        y_copies.append(
            pltpu.make_async_remote_copy(
                src_ref=speed_own, dst_ref=speed_y.at[d], send_sem=y_send.at[d], recv_sem=y_recv.at[d],
                device_id=at(0, d), device_id_type=MESH,
            )
        )
        y_copies[-1].start()

    lanes = lane_ids(width_x)
    per_pack = LANES // GROUP
    packs = columns // per_pack

    def pack(j, carry):
        total = jnp.zeros((width_x, LANES), jnp.float32)
        for i in range(per_pack):
            start = pl.multiple_of((j * per_pack + i) * width_x, width_x)
            turned = pltpu.roll(x_ref[pl.ds(start, width_x), :], (2 + GROUP * i) % LANES, 1)
            total = jnp.where(lanes // GROUP == i, turned, total)
        packed[pl.ds(pl.multiple_of(j * width_x, width_x), width_x), :] = total
        return carry

    lax.fori_loop(0, packs, pack, 0)
    side = [
        remote(packed, from_right, 3, at(0, -1)),
        remote(packed, from_left, 4, at(0, 1)),
    ]
    for copy in side:
        copy.start()

    best = speed_own[...]
    for d in range(1, n_gy):
        y_copies[d - 1].wait()
        best = jnp.maximum(best, speed_y[d])
    speed_row[...] = best
    x_copies = []
    for d in range(1, n_gx):
        x_copies.append(
            pltpu.make_async_remote_copy(
                src_ref=speed_row, dst_ref=speed_x.at[d], send_sem=x_send.at[d], recv_sem=x_recv.at[d],
                device_id=at(d, 0), device_id_type=MESH,
            )
        )
        x_copies[-1].start()

    for copy in side:
        copy.wait()
    has_left = jnp.where(q > 0, 1.0, 0.0)
    has_right = jnp.where(q < n_gy - 1, 1.0, 0.0)
    for j in range(packs):
        here = pl.ds(j * width_x, width_x)
        cols_ref[here, :] = jnp.where(
            lanes % GROUP < 2, from_left[here, :] * has_left, from_right[here, :] * has_right
        )

    for d in range(1, n_gx):
        x_copies[d - 1].wait()
        best = jnp.maximum(best, speed_x[d])
    speed_ref[...] = jnp.broadcast_to(jnp.max(best, keepdims=True), (8, LANES))
    for copy in copies:
        copy.wait()
    corner_ref[...] = corner_ref[...] * has_right


def exchange(mesh, flat, n_fields, levels, width_x):
    n_gx, n_gy = mesh.shape["gx"], mesh.shape["gy"]
    columns = n_fields * levels
    packs = columns * GROUP // LANES
    f32 = jnp.float32
    vmem = pl.BlockSpec(memory_space=pltpu.VMEM)
    shapes = [(2, columns, LANES), (2, columns, LANES), (3 * levels, LANES), (packs * width_x, LANES), (8, LANES)]
    return pl.pallas_call(
        functools.partial(exchange_kernel, n_gx, n_gy, n_fields, levels, width_x),
        out_shape=[jax.ShapeDtypeStruct(s, f32) for s in shapes],
        in_specs=[vmem],
        out_specs=[vmem] * 5,
        scratch_shapes=[
            pltpu.VMEM((4, columns, LANES), f32),
            pltpu.VMEM((packs * width_x, LANES), f32),
            pltpu.VMEM((packs * width_x, LANES), f32),
            pltpu.VMEM((packs * width_x, LANES), f32),
            pltpu.VMEM((8, LANES), f32),
            pltpu.VMEM((8, LANES), f32),
            pltpu.VMEM((n_gy, 8, LANES), f32),
            pltpu.VMEM((n_gx, 8, LANES), f32),
            pltpu.SemaphoreType.DMA((5,)),
            pltpu.SemaphoreType.DMA((5,)),
            pltpu.SemaphoreType.DMA((n_gy,)),
            pltpu.SemaphoreType.DMA((n_gy,)),
            pltpu.SemaphoreType.DMA((n_gx,)),
            pltpu.SemaphoreType.DMA((n_gx,)),
        ],
        compiler_params=pltpu.CompilerParams(
            collective_id=0, has_side_effects=True, vmem_limit_bytes=VMEM_BYTES
        ),
    )(flat)


def unpack_shift(i):
    return LANES - 2 - GROUP * i


def stencil_kernel(
    levels, width_x, x_ref, vel_ref, prior_ref, heights_ref, low_ref, high_ref, cols_ref, speed_ref,
    new_ref, acc_ref, ext,
):
    span = width_x + 16
    per_pack = LANES // GROUP
    step = section_weight * (courant / (speed_ref[0:1, :] + 1e-06))
    zero = jnp.zeros((span, LANES), jnp.float32)
    ext[0:span, :] = zero
    ext[(levels + 1) * span : (levels + 2) * span, :] = zero

    def fill(k, carry):
        start = pl.multiple_of((k + 1) * span + 8, 8)
        ext[pl.ds(start, width_x), :] = x_ref[0, k]
        return carry

    lax.fori_loop(0, levels, fill, 0, unroll=8)
    for d in range(2):
        ext[pl.ds(span + 6 + d, levels, stride=span), :] = low_ref[d]
        ext[pl.ds(span + 8 + width_x + d, levels, stride=span), :] = high_ref[d]
    lanes = lane_ids(width_x)
    heights = heights_ref[...]

    def level(k):
        base = pl.multiple_of((k + 1) * span, 8)
        center = ext[pl.ds(base + 8, width_x), :]

        def along(d):
            return ext[pl.ds(base + 8 + d, width_x), :]

        up = ext[pl.ds(base + span + 8, width_x), :]
        down = ext[pl.ds(base - span + 8, width_x), :]
        edge = cols_ref[0, k // per_pack]
        edge = pltpu.roll(edge, unpack_shift(lax.rem(k, per_pack)), 1)
        right1 = pltpu.roll(jnp.where(lanes == 0, edge, center), LANES - 1, 1)
        right2 = pltpu.roll(jnp.where(lanes <= 1, edge, center), LANES - 2, 1)
        left1 = pltpu.roll(jnp.where(lanes == LANES - 1, edge, center), 1, 1)
        left2 = pltpu.roll(jnp.where(lanes >= LANES - 2, edge, center), 2, 1)
        low1, high1 = along(-1), along(1)
        grad_x = (high1 - low1) * (8.0 / 12.0) - (along(2) - along(-2)) * (1.0 / 12.0)
        grad_y = (right1 - left1) * (8.0 / 12.0) - (right2 - left2) * (1.0 / 12.0)
        grad_z = 0.5 * (up - down)
        laplace = high1 + low1 + right1 + left1 + up + down - 6.0 * center
        tendency = viscosity * laplace - (
            vel_ref[0, k] * grad_x + vel_ref[1, k] * grad_y + vel_ref[2, k] * grad_z
        )
        acc = prior_weight * prior_ref[0, k] + tendency
        fluid = k >= heights
        acc_ref[0, k] = jnp.where(fluid, acc, 0.0)
        new_ref[0, k] = jnp.where(fluid, center + step * acc, 0.0)

    def some(i, carry):
        for j in range(4):
            level(i * 4 + j)
        return carry

    lax.fori_loop(0, levels // 4, some, 0)


def stencil(fields, previous, heights, low, high, cols, speed):
    n_fields, levels, width_x, width_y = fields.shape
    halves = levels * GROUP // LANES
    block = pl.BlockSpec((1, levels, width_x, width_y), lambda f: (f, 0, 0, 0))
    return pl.pallas_call(
        functools.partial(stencil_kernel, levels, width_x),
        grid=(n_fields,),
        out_shape=[jax.ShapeDtypeStruct(fields.shape, jnp.float32)] * 2,
        in_specs=[
            block,
            pl.BlockSpec((3, levels, width_x, width_y), lambda f: (0, 0, 0, 0)),
            block,
            pl.BlockSpec((width_x, width_y), lambda f: (0, 0)),
            pl.BlockSpec((2, levels, LANES), lambda f: (0, f, 0)),
            pl.BlockSpec((2, levels, LANES), lambda f: (0, f, 0)),
            pl.BlockSpec((1, halves, width_x, LANES), lambda f: (f, 0, 0, 0)),
            pl.BlockSpec((8, LANES), lambda f: (0, 0)),
        ],
        out_specs=[block, block],
        scratch_shapes=[pltpu.VMEM(((levels + 2) * (width_x + 16), LANES), jnp.float32)],
        compiler_params=pltpu.CompilerParams(vmem_limit_bytes=VMEM_BYTES),
    )(fields, fields, previous, heights, low, high, cols.reshape(n_fields, halves, width_x, LANES), speed)


def particle_kernel(
    levels, width_x, blocks, tile_ref, col_ref, off_ref, x_ref, high_ref, corner_ref, cols_ref, speed_ref,
    out_ref, table,
):
    per_pack = LANES // GROUP
    lanes = lane_ids(width_x)
    tiles = levels * width_x

    def build(k, carry):
        pack = pl.multiple_of(k // per_pack * width_x, 8)
        base = pl.multiple_of((k * width_x + 1) * 8, 8)
        for s in range(3):
            own = x_ref[s, k]
            edge = cols_ref[pl.ds(s * (levels // per_pack) * width_x + pack, width_x), :]
            edge = pltpu.roll(edge, unpack_shift(lax.rem(k, per_pack)), 1)
            turned = jnp.where(lanes == 0, edge, own)
            table[pl.ds(base + s, width_x, stride=8), :] = own
            table[pl.ds(base - 8 + 3 + s, width_x, stride=8), :] = own
            table[pl.ds(tiles * 8 + base + s, width_x, stride=8), :] = turned
            table[pl.ds(tiles * 8 + base - 8 + 3 + s, width_x, stride=8), :] = turned
        return carry

    lax.fori_loop(0, levels, build, 0)
    first = lane_ids(levels) == 0
    for s in range(3):
        plane = high_ref[0, s * levels : (s + 1) * levels, :]
        corner = corner_ref[s * levels : (s + 1) * levels, :]
        table[pl.ds(width_x * 8 + 3 + s, levels, stride=width_x * 8), :] = plane
        table[pl.ds((tiles + width_x) * 8 + 3 + s, levels, stride=width_x * 8), :] = jnp.where(
            first, corner, plane
        )

    half = LANES // 2
    lanes = lane_ids(8)
    sub = lax.broadcasted_iota(jnp.int32, (8, LANES), 0)
    time_step = courant / (speed_ref[0:1, :] + 1e-06)
    place = lanes % half

    def one(j, carry):
        sums = []
        for h in range(2):
            ids = jnp.broadcast_to(col_ref[pl.ds(2 * j + h, 1), :], (8, LANES))
            got = jnp.zeros((8, LANES), jnp.float32)
            for i in range(half):
                start = pl.multiple_of(tile_ref[j * LANES + h * half + i], 8)
                tile = table[pl.ds(start, 8), :]
                turned = jnp.take_along_axis(tile, ids, axis=1, mode="promise_in_bounds")
                got = jnp.where(place == i, turned, got)
            frac = off_ref[1, pl.ds(j, 1), :]
            other = pltpu.roll(frac, half, 1)
            if h == 0:
                weight = jnp.where(lanes[0:1] < half, 1.0 - frac, other)
            else:
                weight = jnp.where(lanes[0:1] < half, 1.0 - other, frac)
            got = got * weight
            sums.append(got + pltpu.roll(got, half, 1))
        both = jnp.where(lanes < half, sums[0], sums[1])
        frac = off_ref[0, pl.ds(j, 1), :]
        both = both * jnp.where(sub < 3, 1.0 - frac, frac)
        vel = both[0:3] + both[3:6]
        for s in range(3):
            out_ref[s, pl.ds(j, 1), :] = off_ref[s, pl.ds(j, 1), :] + time_step * vel[s : s + 1]
        return carry

    lax.fori_loop(0, blocks, one, 0)


def particles(fields, cells, offsets, high, corner, cols, speed):
    levels, width_x, width_y = fields.shape[1:]
    total = cells.shape[0]
    blocks = total // LANES
    half = LANES // 2
    column = cells % width_y
    tile = (cells // width_y + 1 + jnp.where(column == width_y - 1, levels * width_x, 0)) * 8
    pairs = column.reshape(-1, half)
    pairs = jnp.concatenate([pairs, (pairs + 1) % width_y], axis=1)
    vmem = pl.BlockSpec(memory_space=pltpu.VMEM)
    return pl.pallas_call(
        functools.partial(particle_kernel, levels, width_x, blocks),
        grid=(1,),
        out_shape=jax.ShapeDtypeStruct((3, blocks, LANES), jnp.float32),
        in_specs=[
            pl.BlockSpec(memory_space=pltpu.SMEM),
            vmem,
            vmem,
            pl.BlockSpec((3, levels, width_x, width_y), lambda i: (0, 0, 0, 0)),
            vmem,
            vmem,
            vmem,
            vmem,
        ],
        out_specs=vmem,
        scratch_shapes=[pltpu.VMEM(((2 * levels * width_x + 1) * 8, LANES), jnp.float32)],
        compiler_params=pltpu.CompilerParams(vmem_limit_bytes=VMEM_BYTES),
    )(tile, pairs, offsets.reshape(3, blocks, LANES), fields, high, corner, cols, speed)


def local(mesh, fields, previous, heights, part_cells, part_offsets, cross_counts):
    n_fields, levels, width_x, width_y = fields.shape
    flat = fields.reshape(n_fields * levels * width_x, width_y)
    low, high, corner, cols, speed = exchange(mesh, flat, n_fields, levels, width_x)
    offsets = part_offsets[:, 0, 0]
    counts = cross_counts[0, 0]
    advanced = particles(fields, part_cells[0, 0], offsets, high, corner, cols, speed).reshape(3, -1)
    slots = lax.broadcasted_iota(jnp.int32, (CAP,), 0)
    right_block = advanced[:, P_KEEP : P_KEEP + CAP] * (slots < counts[0]).astype(jnp.float32)
    left_block = advanced[:, P_KEEP + CAP :] * (slots < counts[1]).astype(jnp.float32)
    n_gx = mesh.shape["gx"]
    from_left = lax.ppermute(right_block, "gx", [(i, (i + 1) % n_gx) for i in range(n_gx)])
    from_right = lax.ppermute(left_block, "gx", [((i + 1) % n_gx, i) for i in range(n_gx)])
    updated, accumulated = stencil(fields, previous, heights, low, high, cols, speed)
    part_moved = jnp.concatenate([advanced[:, :P_KEEP], from_left, from_right], axis=-1)
    return (updated, accumulated, part_moved.reshape(3, 1, 1, -1))


def solution(mesh):
    placed = (
        P(None, None, "gx", "gy"),
        P(None, None, "gx", "gy"),
        P("gx", "gy"),
        P("gx", "gy", None),
        P(None, "gx", "gy", None),
        P("gx", "gy", None),
    )
    return jax.shard_map(
        functools.partial(local, mesh),
        mesh=mesh,
        in_specs=placed,
        out_specs=(P(None, None, "gx", "gy"), P(None, None, "gx", "gy"), P(None, "gx", "gy", None)),
        check_vma=False,
    )
```

time: 290 us -> 85.3 us (0.29)
  matrix products: 97.2 us -> 0 us
  local copies, waits for them, and re-layouts: 80.1 us -> 5.86 us
  Pallas kernels: 0 us -> 70.7 us
  other arithmetic: 50.7 us -> 4.7 us
  blocking collectives: 42.4 us -> 0 us
  starting transfers between devices: 14.3 us -> 2.85 us
    dot_general x9 -> x0, matrix products: 97.2 us -> none  [one_block(): jnp.dot(row_weight, vel_table, precision=lax.Precision.HIGHEST, preferred...]
    pallas_call x0 -> x3, Pallas kernels: none -> 70.7 us  [the longest x1 29 us: particles(): pl.pallas_call(functools.partial(particle_kernel, levels, width_x, blocks...]
    pmax x1 -> x0, blocking collectives: 42.4 us -> none  [local(): fastest = lax.pmax(speeds, ('gx', 'gy'))]
    unnamed x70 -> x16, local copies, waits for them, and re-layouts: 29.6 us -> 3.82 us
    reshape x10 -> x1, local copies, waits for them, and re-layouts: 19.9 us -> 0.72 us  [local(): return (updated, accumulated, part_moved.reshape(3, 1, 1, -1))]
    unnamed x9 -> x1, other arithmetic: 16.3 us -> 1.5 us
    reduce_sum x9 -> x0, other arithmetic: 11.5 us -> none  [one_block(): return jnp.sum(picked * col_weight[:, None, :], axis=2)]
    ppermute x6 -> x2, starting transfers between devices: 14.3 us -> 2.85 us  [the longest x1 2.85 us: local(): lax.ppermute(left_block, 'gx', [((i + 1) % n_gx, i) for i in range(n_gx)])]
  transfers between devices with their start and end apart: 6 -> 2, of which waited for: 0 -> 0; matrix products, arithmetic and copies ran while one was open for 19% -> 0% of each run, Pallas kernels for 0% -> 21%
where the time goes in v1:
time: 85.3 us; the launch traced here: 84.9 us
  Pallas kernels  70.7 us (83%)
  local copies, waits for them, and re-layouts  5.86 us (7%)
  other arithmetic  4.7 us (6%)
  starting transfers between devices  2.85 us (3%)
    pallas_call x1, Pallas kernels, particles(): pl.pallas_call(functools.partial(particle_kernel, levels, width_x, blocks...  29 us
    pallas_call x1, Pallas kernels, exchange(): pl.pallas_call(functools.partial(exchange_kernel, n_gx, n_gy, n_fields, l...  23.9 us
    pallas_call x1, Pallas kernels, stencil(): pl.pallas_call(functools.partial(stencil_kernel, levels, width_x), grid=(...  17.8 us
    unnamed x16, local copies, waits for them, and re-layouts  3.82 us
    ppermute x1, starting transfers between devices, local(): lax.ppermute(left_block, 'gx', [((i + 1) % n_gx, i) for i in range(n_gx)])  2.85 us
  transfers between devices with their start and end apart: 2, of which 0 were waited for; matrix products, arithmetic and copies ran while one was open for 0% of the time, Pallas kernels for 21%

profile of v1, /device:TPU:0, one launch (start us, length us, event | category | flops | bytes accessed | tf_op | source)
XLA Modules:
  0.0 84.9 jit_solution(12912233937302287920)
XLA Ops:
  0.6 0.0 copy-start
  0.6 1.7 %copy-done = f32[5,64,16,128]{3,2,1,0:T(8,128)S(1)} copy-done((f32[5,64,16,128]{3,2,1,0:T(8,128)S(1)}, f32[5,64,16,128]{3,2,1,0:T(8,128)}, u32[]{:S(2)}) %copy-start) | copy-done | bytes 2621464
  2.4 0.0 copy-start.1
  2.4 0.0 copy-start.2
  2.4 23.9 %shard_map.85 = (f32[2,320,128]{2,1,0:T(8,128)S(1)}, f32[2,320,128]{2,1,0:T(8,128)S(1)}, f32[192,128]{1,0:T(8,128)S(1)}, f32[160,128]{1,0:T(8,128)S(1)}, f32[8,128]{1,0:T(8,128)S(1)}) custom-call(f32[5120,128]{1,0:T(8,128)S(1)} %bitcast.10), custom_call_target="tpu_custom_call" | custom-call | tf_op jit(solution)/shard_map/pallas_call | solution.py:150
  26.3 0.0 copy-start.3
  26.3 0.6 copy-done.3
  26.9 0.0 copy-start.5
  26.9 0.8 fusion.4.tile_ref
  27.8 0.5 broadcast.45
  28.3 1.5 %reduce.3 = s32[9216]{0:T(1024)S(1)} reduce(s32[1,1,9216]{2,1,0:T(1,128)} %param.9, s32[]{:T(128)} %broadcast.45), dimensions={0,1}, to_apply=%param.9.reduce_sub_computation.3 | reduce | bytes 73732 | tf_op args[3]
  29.8 0.7 squeeze.13
  30.5 0.0 copy-start.6
  30.5 1.0 %add_select_fusion.1 = (s32[144,64]{1,0:T(8,128)S(1)}, s32[144,64]{1,0:T(8,128)S(1)}) fusion(s32[144,64]{1,0:T(8,128)} %squeeze.13), kind=kLoop, calls=%fused_computation.5 | loop fusion | flops 211968 | bytes 110592 | tf_op jit(solution)/shard_map/jit(remainder)/select_n | solution.py:336
  31.5 0.1 pad_add_fusion.col_ref
  31.5 0.0 copy-done.1
  31.6 0.0 copy-done.2
  31.6 0.0 copy-start.4
  31.6 0.9 %copy-done.4 = f32[192,128]{1,0:T(8,128)S(1)} copy-done((f32[192,128]{1,0:T(8,128)S(1)}, f32[192,128]{1,0:T(8,128)}, u32[]{:S(2)}) %copy-start.4) | copy-done | bytes 98328
  32.5 29.0 %shard_map.87 = f32[3,72,128]{2,1,0:T(8,128)S(1)} custom-call(s32[9216]{0:T(1024)S(1)} %fusion.4.tile_ref, s32[144,128]{1,0:T(8,128)S(1)} %pad_add_fusion.col_ref, f32[3,72,128]{2,1,0:T(8,128)S(1)} %bitcast.13, f32[5,64,16,128]{3,2,1,0:T(8,128)S(1)} %copy-done.1, f32[2,320,128]{2,1,0:T(8,128)S(1)} %get-tuple-element.11.high_ref, f32[192,128]{1,0:T(8,128)S(1)} %copy-done.4, ...), custom_call_target="tpu_custom_call" | custom-call | tf_op jit(solution)/shard_map/pallas_call | solution.py:341
  61.5 0.0 copy-done.6
  61.5 0.6 fusion.10
  62.1 1.3 %fusion.8 = (f32[512]{0:T(512)S(1)}, f32[512]{0:T(512)S(1)}) fusion(s32[]{:T(128)} %bitcast.4, s32[]{:T(128)} %bitcast.5), kind=kLoop, calls=%fused_computation.27 | loop fusion | flops 2048 | bytes 4104 | tf_op jit(solution)/shard_map/convert_element_type | solution.py:369
  63.4 2.8 %collective-permute-start.1 = (f32[3,512]{1,0:T(4,128)S(1)}, f32[3,512]{1,0:T(4,128)S(1)}, u32[]{:S(2)}, u32[]{:S(2)}) collective-permute-start(f32[3,512]{1,0:T(4,128)S(1)} %get-tuple-element.18), channel_id=1, source_target_pairs={{4,0},{8,4},{12,8},{16,12},{20,16},{24,20},{28,24},{0,28},{5,1},{9... | collective-permute-start | bytes 18440 | tf_op jit(solution)/shard_map/ppermute | solution.py:373
  66.3 0.0 collective-permute-start
  66.3 0.0 copy-done.5
  66.3 17.8 %shard_map.86 = (f32[5,64,16,128]{3,2,1,0:T(8,128)}, f32[5,64,16,128]{3,2,1,0:T(8,128)}) custom-call(f32[5,64,16,128]{3,2,1,0:T(8,128)S(1)} %copy-done.1, f32[5,64,16,128]{3,2,1,0:T(8,128)S(1)} %copy-done.1, f32[5,64,16,128]{3,2,1,0:T(8,128)} %prior_ref.1, s32[16,128]{1,0:T(8,128)S(1)} %copy-done.5, f32[2,320,128]{2,1,0:T(8,128)S(1)} %get-tuple-element.10.low_ref, ...), custom_call_target="tpu_custom_call" | custom-call | tf_op jit(solution)/shard_map/pallas_call | solution.py:244
  84.1 0.0 collective-permute-done.1
  84.1 0.0 collective-permute-done
  84.2 0.7 reshape.37
  (4 shorter events, 0.1 us)
Async XLA Ops:
  0.6 1.7 %copy-start = (f32[5,64,16,128]{3,2,1,0:T(8,128)S(1)}, f32[5,64,16,128]{3,2,1,0:T(8,128)}, u32[]{:S(2)}) copy-start(f32[5,64,16,128]{3,2,1,0:T(8,128)} %x_ref.3) | copy-start | bytes 7864324
  2.4 29.2 %copy-start.1 = (f32[5,64,16,128]{3,2,1,0:T(8,128)S(1)}, f32[5,64,16,128]{3,2,1,0:T(8,128)}, u32[]{:S(2)}) copy-start(f32[5,64,16,128]{3,2,1,0:T(8,128)} %x_ref.3) | copy-start | bytes 7864324
  2.4 29.2 %copy-start.2 = (f32[3,1,1,9216]{3,2,1,0:T(1,128)S(1)}, f32[3,1,1,9216]{3,2,1,0:T(1,128)}, u32[]{:S(2)}) copy-start(f32[3,1,1,9216]{3,2,1,0:T(1,128)} %param.10) | copy-start | bytes 331780
  26.3 0.6 copy-start.3
  26.9 39.4 %copy-start.5 = (s32[16,128]{1,0:T(8,128)S(1)}, s32[16,128]{1,0:T(8,128)}, u32[]{:S(2)}) copy-start(s32[16,128]{1,0:T(8,128)} %heights_ref.1) | copy-start | bytes 24580
  30.5 31.0 %copy-start.6 = (s32[1,1,2]{2,1,0:T(1,128)S(1)}, s32[1,1,2]{2,1,0:T(1,128)}, u32[]{:S(2)}) copy-start(s32[1,1,2]{2,1,0:T(1,128)} %param.11) | copy-start | bytes 28
  31.6 0.9 %copy-start.4 = (f32[192,128]{1,0:T(8,128)S(1)}, f32[192,128]{1,0:T(8,128)}, u32[]{:S(2)}) copy-start(f32[192,128]{1,0:T(8,128)} %copy-done.3) | copy-start | bytes 294916
  63.4 20.7 %collective-permute-start.1 = (f32[3,512]{1,0:T(4,128)S(1)}, f32[3,512]{1,0:T(4,128)S(1)}, u32[]{:S(2)}, u32[]{:S(2)}) collective-permute-start(f32[3,512]{1,0:T(4,128)S(1)} %get-tuple-element.18), channel_id=1, source_target_pairs={{4,0},{8,4},{12,8},{16,12},{20,16},{24,20},{28,24},{0,28},{5,1},{9... | collective-permute-start | bytes 18440 | tf_op jit(solution)/shard_map/ppermute | solution.py:373
  66.3 17.9 %collective-permute-start = (f32[3,512]{1,0:T(4,128)S(1)}, f32[3,512]{1,0:T(4,128)S(1)}, u32[]{:S(2)}, u32[]{:S(2)}) collective-permute-start(f32[3,512]{1,0:T(4,128)S(1)} %get-tuple-element.17), channel_id=1, source_target_pairs={{0,4},{4,8},{8,12},{12,16},{16,20},{20,24},{24,28},{28,0},{1,5},{5... | collective-permute-start | bytes 18440 | tf_op jit(solution)/shard_map/ppermute | solution.py:372

commit v2 on v1

v2 whole, which is shorter than its diff:
```python
import functools

import jax
import jax.numpy as jnp
from jax import lax
from jax.experimental import pallas as pl
from jax.experimental.pallas import tpu as pltpu
from jax.sharding import PartitionSpec as P

P_KEEP = 8192
CAP = 512
LANES = 128
GROUP = 4
VMEM_BYTES = 50 * 2**20

courant = 0.9
viscosity = 0.1
prior_weight = -5.0 / 9.0
section_weight = 15.0 / 16.0

MESH = pl.DeviceIdType.MESH


def lane_ids(rows):
    return lax.broadcasted_iota(jnp.int32, (rows, LANES), 1)


def unpack_shift(i):
    return LANES - 2 - GROUP * i


def advance_kernel(
    n_gx, n_gy, n_fields, levels, width_x, blocks,
    tile_ref, counts_ref, col_ref, off_ref, x_hbm,
    low_ref, high_ref, cols_ref, speed_ref, out_ref,
    x_ref, table, planes, corner_ref, packed, from_left, from_right, speed_own, speed_row, speed_y, speed_x,
    cross_own, cross_in,
    load_sem, send_sems, recv_sems, y_send, y_recv, x_send, x_recv,
):
    p = lax.axis_index("gx")
    q = lax.axis_index("gy")

    def at(dp, dq):
        return (lax.rem(p + dp + n_gx, n_gx), lax.rem(q + dq + n_gy, n_gy))

    load = pltpu.make_async_copy(x_hbm, x_ref, load_sem)
    load.start()
    barrier = pltpu.get_barrier_semaphore()
    peers = [at(d, 0) for d in range(1, n_gx)] + [at(0, d) for d in range(1, n_gy)]
    peers += [at(-1, -1), at(1, 1)]
    for peer in peers:
        pl.semaphore_signal(barrier, inc=1, device_id=peer, device_id_type=MESH)

    columns = n_fields * levels
    load.wait()
    for slot, row in enumerate((0, 1, width_x - 2, width_x - 1)):
        planes[slot] = x_ref[pl.ds(row, columns, stride=width_x), :]
    pl.semaphore_wait(barrier, len(peers))

    def remote(src, dst, index, peer):
        return pltpu.make_async_remote_copy(
            src_ref=src, dst_ref=dst, send_sem=send_sems.at[index], recv_sem=recv_sems.at[index],
            device_id=peer, device_id_type=MESH,
        )

    used = 3 * levels
    near = [
        remote(planes.at[0, pl.ds(0, used)], high_ref.at[0, pl.ds(0, used)], 0, at(-1, 0)),
        remote(planes.at[0, pl.ds(0, used)], corner_ref, 1, at(-1, -1)),
    ]
    for copy in near:
        copy.start()

    rows = levels * width_x

    def fastest_rows(i, best):
        start = pl.multiple_of(i * 64, 64)
        total = (
            jnp.abs(x_ref[pl.ds(start, 64), :])
            + jnp.abs(x_ref[pl.ds(rows + start, 64), :])
            + jnp.abs(x_ref[pl.ds(2 * rows + start, 64), :])
        )
        return jnp.maximum(best, jnp.max(total.reshape(8, 8, LANES), axis=0))

    speed_own[...] = lax.fori_loop(0, rows // 64, fastest_rows, jnp.zeros((8, LANES), jnp.float32))

    y_copies = []
    for d in range(1, n_gy):
        y_copies.append(
            pltpu.make_async_remote_copy(
                src_ref=speed_own, dst_ref=speed_y.at[d], send_sem=y_send.at[d], recv_sem=y_recv.at[d],
                device_id=at(0, d), device_id_type=MESH,
            )
        )
        y_copies[-1].start()

    lanes = lane_ids(width_x)
    per_pack = LANES // GROUP
    packs = columns // per_pack

    def pack(j, carry):
        total = jnp.zeros((width_x, LANES), jnp.float32)
        for i in range(per_pack):
            start = pl.multiple_of((j * per_pack + i) * width_x, width_x)
            turned = pltpu.roll(x_ref[pl.ds(start, width_x), :], (2 + GROUP * i) % LANES, 1)
            total = jnp.where(lanes // GROUP == i, turned, total)
        packed[pl.ds(pl.multiple_of(j * width_x, width_x), width_x), :] = total
        return carry

    lax.fori_loop(0, packs, pack, 0)
    side = [
        remote(packed, from_right, 2, at(0, -1)),
        remote(packed, from_left, 3, at(0, 1)),
    ]
    for copy in side:
        copy.start()
    rest = columns - used
    far = [
        remote(planes.at[0, pl.ds(used, rest)], high_ref.at[0, pl.ds(used, rest)], 4, at(-1, 0)),
        remote(planes.at[1], high_ref.at[1], 5, at(-1, 0)),
        remote(planes.at[pl.ds(2, 2)], low_ref, 6, at(1, 0)),
    ]

    best = speed_own[...]
    for d in range(1, n_gy):
        y_copies[d - 1].wait()
        best = jnp.maximum(best, speed_y[d])
    speed_row[...] = best
    x_copies = []
    for d in range(1, n_gx):
        x_copies.append(
            pltpu.make_async_remote_copy(
                src_ref=speed_row, dst_ref=speed_x.at[d], send_sem=x_send.at[d], recv_sem=x_recv.at[d],
                device_id=at(d, 0), device_id_type=MESH,
            )
        )
        x_copies[-1].start()
    for copy in far:
        copy.start()

    def build_own(k, carry):
        base = k * width_x + 1
        for s in range(3):
            own = x_ref[pl.ds(pl.multiple_of(s * rows + k * width_x, 8), width_x), :]
            table[pl.ds(base, width_x), s, :] = own
            table[pl.ds(base - 1, width_x), 3 + s, :] = own
        return carry

    lax.fori_loop(0, levels, build_own, 0, unroll=2)

    for copy in side:
        copy.wait()
    has_left = jnp.where(q > 0, 1.0, 0.0)
    has_right = jnp.where(q < n_gy - 1, 1.0, 0.0)
    for j in range(packs):
        here = pl.ds(j * width_x, width_x)
        cols_ref[here, :] = jnp.where(
            lanes % GROUP < 2, from_left[here, :] * has_left, from_right[here, :] * has_right
        )

    def build_turned(j, carry):
        for i in range(per_pack):
            k = j * per_pack + i
            base = k * width_x + 1 + rows
            for s in range(3):
                own = x_ref[pl.ds(pl.multiple_of(s * rows + k * width_x, 8), width_x), :]
                start = pl.multiple_of((s * (levels // per_pack) + j) * width_x, 8)
                edge = pltpu.roll(cols_ref[pl.ds(start, width_x), :], unpack_shift(i), 1)
                turned = jnp.where(lanes == 0, edge, own)
                table[pl.ds(base, width_x), s, :] = turned
                table[pl.ds(base - 1, width_x), 3 + s, :] = turned
        return carry

    lax.fori_loop(0, levels // per_pack, build_turned, 0)
    for copy in near:
        copy.wait()
    first = lane_ids(levels) == 0
    for s in range(3):
        plane = high_ref[0, s * levels : (s + 1) * levels, :]
        corner = corner_ref[s * levels : (s + 1) * levels, :] * has_right
        table[pl.ds(width_x, levels, stride=width_x), 3 + s, :] = plane
        table[pl.ds(rows + width_x, levels, stride=width_x), 3 + s, :] = jnp.where(
            first, corner, plane
        )

    for d in range(1, n_gx):
        x_copies[d - 1].wait()
        best = jnp.maximum(best, speed_x[d])
    fastest = jnp.broadcast_to(jnp.max(best, keepdims=True), (8, LANES))
    speed_ref[...] = fastest
    time_step = courant / (fastest[0:1, :] + 1e-06)

    half = LANES // 2
    lanes = lane_ids(8)
    sub = lax.broadcasted_iota(jnp.int32, (8, LANES), 0)
    place = lanes % half

    def one(j, carry):
        sums = []
        for h in range(2):
            ids = jnp.broadcast_to(col_ref[pl.ds(2 * j + h, 1), :], (8, LANES))
            got = jnp.zeros((8, LANES), jnp.float32)
            for i in range(half):
                tile = table[tile_ref[j * LANES + h * half + i]]
                turned = jnp.take_along_axis(tile, ids, axis=1, mode="promise_in_bounds")
                got = jnp.where(place == i, turned, got)
            frac = off_ref[1, pl.ds(j, 1), :]
            other = pltpu.roll(frac, half, 1)
            if h == 0:
                weight = jnp.where(lanes[0:1] < half, 1.0 - frac, other)
            else:
                weight = jnp.where(lanes[0:1] < half, 1.0 - other, frac)
            got = got * weight
            sums.append(got + pltpu.roll(got, half, 1))
        both = jnp.where(lanes < half, sums[0], sums[1])
        frac = off_ref[0, pl.ds(j, 1), :]
        both = both * jnp.where(sub < 3, 1.0 - frac, frac)
        vel = both[0:3] + both[3:6]
        for s in range(3):
            out_ref[s, pl.ds(j, 1), :] = off_ref[s, pl.ds(j, 1), :] + time_step * vel[s : s + 1]
        return carry

    kept, cap = P_KEEP // LANES, CAP // LANES
    lax.fori_loop(kept, blocks, one, 0)
    slots = lax.broadcasted_iota(jnp.int32, (cap, LANES), 0) * LANES + lane_ids(cap)
    crossing = []
    for way in range(2):
        live = jnp.where(slots < counts_ref[way], 1.0, 0.0)
        for s in range(3):
            cross_own[way, s] = out_ref[s, pl.ds(kept + way * cap, cap), :] * live
        crossing.append(remote(cross_own.at[way], cross_in.at[way], 7 + way, at(1 - 2 * way, 0)))
        crossing[-1].start()
    lax.fori_loop(0, kept, one, 0)
    for way in range(2):
        crossing[way].wait()
        for s in range(3):
            out_ref[s, pl.ds(kept + way * cap, cap), :] = cross_in[way, s]
    for copy in far:
        copy.wait()


def advance(mesh, fields, cells, offsets, counts):
    n_gx, n_gy = mesh.shape["gx"], mesh.shape["gy"]
    n_fields, levels, width_x, width_y = fields.shape
    columns = n_fields * levels
    packed = (columns * GROUP // LANES * width_x, LANES)
    blocks = cells.shape[0] // LANES
    half = LANES // 2
    column = cells % width_y
    tile = cells // width_y + 1 + jnp.where(column == width_y - 1, levels * width_x, 0)
    pairs = column.reshape(-1, half)
    pairs = jnp.concatenate([pairs, (pairs + 1) % width_y], axis=1)
    f32 = jnp.float32
    vmem = pl.BlockSpec(memory_space=pltpu.VMEM)
    smem = pl.BlockSpec(memory_space=pltpu.SMEM)
    shapes = [(2, columns, LANES), (2, columns, LANES), packed, (8, LANES), (3, blocks, LANES)]
    return pl.pallas_call(
        functools.partial(advance_kernel, n_gx, n_gy, n_fields, levels, width_x, blocks),
        out_shape=[jax.ShapeDtypeStruct(s, f32) for s in shapes],
        in_specs=[smem, smem, vmem, vmem, pl.BlockSpec(memory_space=pl.ANY)],
        out_specs=[vmem] * 5,
        scratch_shapes=[
            pltpu.VMEM((columns * width_x, LANES), f32),
            pltpu.VMEM((2 * levels * width_x + 1, 8, LANES), f32),
            pltpu.VMEM((4, columns, LANES), f32),
            pltpu.VMEM((3 * levels, LANES), f32),
            pltpu.VMEM(packed, f32),
            pltpu.VMEM(packed, f32),
            pltpu.VMEM(packed, f32),
            pltpu.VMEM((8, LANES), f32),
            pltpu.VMEM((8, LANES), f32),
            pltpu.VMEM((n_gy, 8, LANES), f32),
            pltpu.VMEM((n_gx, 8, LANES), f32),
            pltpu.VMEM((2, 3, CAP // LANES, LANES), f32),
            pltpu.VMEM((2, 3, CAP // LANES, LANES), f32),
            pltpu.SemaphoreType.DMA,
            pltpu.SemaphoreType.DMA((9,)),
            pltpu.SemaphoreType.DMA((9,)),
            pltpu.SemaphoreType.DMA((n_gy,)),
            pltpu.SemaphoreType.DMA((n_gy,)),
            pltpu.SemaphoreType.DMA((n_gx,)),
            pltpu.SemaphoreType.DMA((n_gx,)),
        ],
        compiler_params=pltpu.CompilerParams(
            collective_id=0, has_side_effects=True, vmem_limit_bytes=VMEM_BYTES
        ),
    )(tile, counts, pairs, offsets.reshape(3, blocks, LANES), fields.reshape(-1, width_y))


def stencil_kernel(
    levels, width_x, x_ref, vel_ref, prior_ref, heights_ref, low_ref, high_ref, cols_ref, speed_ref,
    new_ref, acc_ref, ext,
):
    span = width_x + 16
    per_pack = LANES // GROUP
    step = section_weight * (courant / (speed_ref[0:1, :] + 1e-06))
    zero = jnp.zeros((span, LANES), jnp.float32)
    ext[0:span, :] = zero
    ext[(levels + 1) * span : (levels + 2) * span, :] = zero

    def fill(k, carry):
        start = pl.multiple_of((k + 1) * span + 8, 8)
        ext[pl.ds(start, width_x), :] = x_ref[0, k]
        return carry

    lax.fori_loop(0, levels, fill, 0, unroll=8)
    for d in range(2):
        ext[pl.ds(span + 6 + d, levels, stride=span), :] = low_ref[d]
        ext[pl.ds(span + 8 + width_x + d, levels, stride=span), :] = high_ref[d]
    lanes = lane_ids(width_x)
    heights = heights_ref[...]

    def level(half, i):
        k = half * per_pack + i
        base = pl.multiple_of((k + 1) * span, 8)
        center = ext[pl.ds(base + 8, width_x), :]

        def along(d):
            return ext[pl.ds(base + 8 + d, width_x), :]

        up = ext[pl.ds(base + span + 8, width_x), :]
        down = ext[pl.ds(base - span + 8, width_x), :]
        edge = pltpu.roll(cols_ref[0, half], unpack_shift(i), 1)
        right1 = pltpu.roll(jnp.where(lanes == 0, edge, center), LANES - 1, 1)
        right2 = pltpu.roll(jnp.where(lanes <= 1, edge, center), LANES - 2, 1)
        left1 = pltpu.roll(jnp.where(lanes == LANES - 1, edge, center), 1, 1)
        left2 = pltpu.roll(jnp.where(lanes >= LANES - 2, edge, center), 2, 1)
        low1, high1 = along(-1), along(1)
        grad_x = (high1 - low1) * (8.0 / 12.0) - (along(2) - along(-2)) * (1.0 / 12.0)
        grad_y = (right1 - left1) * (8.0 / 12.0) - (right2 - left2) * (1.0 / 12.0)
        grad_z = 0.5 * (up - down)
        laplace = high1 + low1 + right1 + left1 + up + down - 6.0 * center
        tendency = viscosity * laplace - (
            vel_ref[0, k] * grad_x + vel_ref[1, k] * grad_y + vel_ref[2, k] * grad_z
        )
        acc = prior_weight * prior_ref[0, k] + tendency
        fluid = k >= heights
        acc_ref[0, k] = jnp.where(fluid, acc, 0.0)
        new_ref[0, k] = jnp.where(fluid, center + step * acc, 0.0)

    def some(half, carry):
        for i in range(per_pack):
            level(half, i)
        return carry

    lax.fori_loop(0, levels // per_pack, some, 0)


def stencil(fields, previous, heights, low, high, cols, speed):
    n_fields, levels, width_x, width_y = fields.shape
    halves = levels * GROUP // LANES
    block = pl.BlockSpec((1, levels, width_x, width_y), lambda f: (f, 0, 0, 0))
    return pl.pallas_call(
        functools.partial(stencil_kernel, levels, width_x),
        grid=(n_fields,),
        out_shape=[jax.ShapeDtypeStruct(fields.shape, jnp.float32)] * 2,
        in_specs=[
            block,
            pl.BlockSpec((3, levels, width_x, width_y), lambda f: (0, 0, 0, 0)),
            block,
            pl.BlockSpec((width_x, width_y), lambda f: (0, 0)),
            pl.BlockSpec((2, levels, LANES), lambda f: (0, f, 0)),
            pl.BlockSpec((2, levels, LANES), lambda f: (0, f, 0)),
            pl.BlockSpec((1, halves, width_x, LANES), lambda f: (f, 0, 0, 0)),
            pl.BlockSpec((8, LANES), lambda f: (0, 0)),
        ],
        out_specs=[block, block],
        scratch_shapes=[pltpu.VMEM(((levels + 2) * (width_x + 16), LANES), jnp.float32)],
        compiler_params=pltpu.CompilerParams(vmem_limit_bytes=VMEM_BYTES),
    )(fields, fields, previous, heights, low, high, cols.reshape(n_fields, halves, width_x, LANES), speed)


def local(mesh, fields, previous, heights, part_cells, part_offsets, cross_counts):
    low, high, cols, speed, moved = advance(
        mesh, fields, part_cells[0, 0], part_offsets[:, 0, 0], cross_counts[0, 0]
    )
    updated, accumulated = stencil(fields, previous, heights, low, high, cols, speed)
    return (updated, accumulated, moved.reshape(3, 1, 1, -1))


def solution(mesh):
    placed = (
        P(None, None, "gx", "gy"),
        P(None, None, "gx", "gy"),
        P("gx", "gy"),
        P("gx", "gy", None),
        P(None, "gx", "gy", None),
        P("gx", "gy", None),
    )
    return jax.shard_map(
        functools.partial(local, mesh),
        mesh=mesh,
        in_specs=placed,
        out_specs=(P(None, None, "gx", "gy"), P(None, None, "gx", "gy"), P(None, "gx", "gy", None)),
        check_vma=False,
    )
```

time: 85.3 us -> 72.4 us (0.85)
  Pallas kernels: 70.7 us -> 64.3 us
  starting transfers between devices: 2.85 us -> 0 us
  other arithmetic: 4.7 us -> 2.46 us
  local copies, waits for them, and re-layouts: 5.86 us -> 4.53 us
    pallas_call x2 -> x1, Pallas kernels: 52.9 us -> 44.2 us  [advance(): pl.pallas_call(functools.partial(advance_kernel, n_gx, n_gy, n_fields, le...]
    ppermute x2 -> x0, starting transfers between devices: 2.85 us -> none  [the longest x1 2.85 us: local(): lax.ppermute(left_block, 'gx', [((i + 1) % n_gx, i) for i in range(n_gx)])]
    pallas_call x1, Pallas kernels: 17.8 us -> 20.2 us  [stencil(): pl.pallas_call(functools.partial(stencil_kernel, levels, width_x), grid=(...]
    convert_element_type x1 -> x0, other arithmetic: 1.29 us -> none  [local(): (slots < counts[0]).astype(jnp.float32)]
    select_n x1, other arithmetic: 0.96 us -> 0.06 us  [advance(): column = cells % width_y]
    unnamed x16 -> x12, local copies, waits for them, and re-layouts: 3.82 us -> 4.45 us
  transfers between devices with their start and end apart: 2 -> 0, of which waited for: 0 -> 0; matrix products, arithmetic and copies ran while one was open for 0% -> 0% of each run, Pallas kernels for 21% -> 0%
where the time goes in v2:
time: 72.4 us; the launch traced here: 72 us
  Pallas kernels  64.3 us (89%)
  local copies, waits for them, and re-layouts  4.53 us (6%)
  other arithmetic  2.46 us (3%)
    pallas_call x1, Pallas kernels, advance(): pl.pallas_call(functools.partial(advance_kernel, n_gx, n_gy, n_fields, le...  44.2 us
    pallas_call x1, Pallas kernels, stencil(): pl.pallas_call(functools.partial(stencil_kernel, levels, width_x), grid=(...  20.2 us
    unnamed x12, local copies, waits for them, and re-layouts  4.45 us
    unnamed x1, other arithmetic  1.5 us

profile of v2, /device:TPU:0, one launch (start us, length us, event | category | flops | bytes accessed | tf_op | source)
XLA Modules:
  0.0 72.0 jit_solution(12293121602323701374)
XLA Ops:
  0.6 0.0 copy-start.3
  0.6 0.5 broadcast.37
  1.2 1.5 %reduce.3 = s32[9216]{0:T(1024)S(1)} reduce(s32[1,1,9216]{2,1,0:T(1,128)} %param.9, s32[]{:T(128)} %broadcast.37), dimensions={0,1}, to_apply=%param.9.reduce_sub_computation.3 | reduce | bytes 73732 | tf_op args[3]
  2.7 0.1 squeeze.10
  2.7 0.8 %fusion.3.tile_ref = s32[9216]{0:T(1024)S(1)} fusion(s32[9216]{0:T(1024)} %bitcast.11), kind=kLoop, calls=%fused_computation.15 | loop fusion | flops 211968 | bytes 73728 | tf_op jit(solution)/shard_map/add | solution.py:250
  3.5 0.1 add_select_fusion.1
  3.6 0.1 pad_add_fusion.col_ref
  3.7 0.0 copy-start
  3.7 1.7 %copy-done = f32[5,64,16,128]{3,2,1,0:T(8,128)S(1)} copy-done((f32[5,64,16,128]{3,2,1,0:T(8,128)S(1)}, f32[5,64,16,128]{3,2,1,0:T(8,128)}, u32[]{:S(2)}) %copy-start) | copy-done | bytes 2621464
  5.5 0.0 copy-start.2
  5.5 0.9 %copy-done.2 = f32[3,1,1,9216]{3,2,1,0:T(1,128)S(1)} copy-done((f32[3,1,1,9216]{3,2,1,0:T(1,128)S(1)}, f32[3,1,1,9216]{3,2,1,0:T(1,128)}, u32[]{:S(2)}) %copy-start.2) | copy-done | bytes 110616
  6.4 0.0 copy-start.4
  6.4 0.7 copy-done.4
  7.0 0.0 copy-start.1
  7.0 44.2 %shard_map.85 = (f32[2,320,128]{2,1,0:T(8,128)S(1)}, f32[2,320,128]{2,1,0:T(8,128)S(1)}, f32[160,128]{1,0:T(8,128)S(1)}, f32[8,128]{1,0:T(8,128)S(1)}, f32[3,72,128]{2,1,0:T(8,128)S(1)}) custom-call(s32[9216]{0:T(1024)S(1)} %fusion.3.tile_ref, s32[2]{0:T(128)S(1)} %bitcast.10, s32[144,128]{1,0:T(8,128)S(1)} %pad_add_fusion.col_ref, ...), custom_call_target="tpu_custom_call" | custom-call | tf_op jit(solution)/shard_map/pallas_call | solution.py:257
  51.2 0.0 copy-done.3
  51.2 0.0 copy-done.1
  51.2 20.2 %shard_map.86 = (f32[5,64,16,128]{3,2,1,0:T(8,128)}, f32[5,64,16,128]{3,2,1,0:T(8,128)}) custom-call(f32[5,64,16,128]{3,2,1,0:T(8,128)S(1)} %copy-done.1, f32[5,64,16,128]{3,2,1,0:T(8,128)S(1)} %copy-done.1, f32[5,64,16,128]{3,2,1,0:T(8,128)} %prior_ref.1, s32[16,128]{1,0:T(8,128)S(1)} %copy-done.3, f32[2,320,128]{2,1,0:T(8,128)S(1)} %get-tuple-element.10.low_ref, ...), custom_call_target="tpu_custom_call" | custom-call | tf_op jit(solution)/shard_map/pallas_call | solution.py:353
  71.4 0.6 copy.12
Async XLA Ops:
  0.6 50.5 %copy-start.3 = (s32[16,128]{1,0:T(8,128)S(1)}, s32[16,128]{1,0:T(8,128)}, u32[]{:S(2)}) copy-start(s32[16,128]{1,0:T(8,128)} %heights_ref.1) | copy-start | bytes 24580
  3.7 1.7 %copy-start = (f32[5,64,16,128]{3,2,1,0:T(8,128)S(1)}, f32[5,64,16,128]{3,2,1,0:T(8,128)}, u32[]{:S(2)}) copy-start(f32[5,64,16,128]{3,2,1,0:T(8,128)} %vel_ref.1) | copy-start | bytes 7864324
  5.5 0.9 %copy-start.2 = (f32[3,1,1,9216]{3,2,1,0:T(1,128)S(1)}, f32[3,1,1,9216]{3,2,1,0:T(1,128)}, u32[]{:S(2)}) copy-start(f32[3,1,1,9216]{3,2,1,0:T(1,128)} %param.10) | copy-start | bytes 331780
  6.4 0.7 copy-start.4
  7.0 44.2 %copy-start.1 = (f32[5,64,16,128]{3,2,1,0:T(8,128)S(1)}, f32[5,64,16,128]{3,2,1,0:T(8,128)}, u32[]{:S(2)}) copy-start(f32[5,64,16,128]{3,2,1,0:T(8,128)} %vel_ref.1) | copy-start | bytes 7864324

commit v3 on v2

--- a/solution.py
+++ b/solution.py
@@ -11,7 +11,7 @@
 CAP = 512
 LANES = 128
 GROUP = 4
-VMEM_BYTES = 50 * 2**20
+VMEM_BYTES = 60 * 2**20
 
 courant = 0.9
 viscosity = 0.1
@@ -31,7 +31,7 @@
 
 def advance_kernel(
     n_gx, n_gy, n_fields, levels, width_x, blocks,
-    tile_ref, counts_ref, col_ref, off_ref, x_hbm,
+    tile_ref, counts_ref, cell_ref, off_ref, x_hbm,
     low_ref, high_ref, cols_ref, speed_ref, out_ref,
     x_ref, table, planes, corner_ref, packed, from_left, from_right, speed_own, speed_row, speed_y, speed_x,
     cross_own, cross_in,
@@ -197,44 +197,50 @@
 
     def one(j, carry):
         sums = []
+        here = pl.ds(pl.multiple_of(j * LANES, LANES), LANES)
+        column = cell_ref[0, :, here] % LANES
+        column_other = pltpu.roll(column, half, 1)
+        frac = off_ref[1, 0, :, here]
+        other = pltpu.roll(frac, half, 1)
+        early = lanes[0:1] < half
         for h in range(2):
-            ids = jnp.broadcast_to(col_ref[pl.ds(2 * j + h, 1), :], (8, LANES))
+            if h == 0:
+                ids = jnp.where(early, column, (column_other + 1) % LANES)
+                weight = jnp.where(early, 1.0 - frac, other)
+            else:
+                ids = jnp.where(early, column_other, (column + 1) % LANES)
+                weight = jnp.where(early, 1.0 - other, frac)
+            ids = jnp.broadcast_to(ids, (8, LANES))
             got = jnp.zeros((8, LANES), jnp.float32)
             for i in range(half):
-                tile = table[tile_ref[j * LANES + h * half + i]]
+                tile = table[tile_ref[0, 0, j * LANES + h * half + i]]
                 turned = jnp.take_along_axis(tile, ids, axis=1, mode="promise_in_bounds")
                 got = jnp.where(place == i, turned, got)
-            frac = off_ref[1, pl.ds(j, 1), :]
-            other = pltpu.roll(frac, half, 1)
-            if h == 0:
-                weight = jnp.where(lanes[0:1] < half, 1.0 - frac, other)
-            else:
-                weight = jnp.where(lanes[0:1] < half, 1.0 - other, frac)
             got = got * weight
             sums.append(got + pltpu.roll(got, half, 1))
         both = jnp.where(lanes < half, sums[0], sums[1])
-        frac = off_ref[0, pl.ds(j, 1), :]
+        frac = off_ref[0, 0, :, here]
         both = both * jnp.where(sub < 3, 1.0 - frac, frac)
         vel = both[0:3] + both[3:6]
         for s in range(3):
-            out_ref[s, pl.ds(j, 1), :] = off_ref[s, pl.ds(j, 1), :] + time_step * vel[s : s + 1]
+            out_ref[s, 0, :, here] = off_ref[s, 0, :, here] + time_step * vel[s : s + 1]
         return carry
 
-    kept, cap = P_KEEP // LANES, CAP // LANES
+    kept = P_KEEP // LANES
     lax.fori_loop(kept, blocks, one, 0)
-    slots = lax.broadcasted_iota(jnp.int32, (cap, LANES), 0) * LANES + lane_ids(cap)
+    slots = lax.broadcasted_iota(jnp.int32, (1, CAP), 1)
     crossing = []
     for way in range(2):
-        live = jnp.where(slots < counts_ref[way], 1.0, 0.0)
+        live = jnp.where(slots < counts_ref[0, 0, way], 1.0, 0.0)
         for s in range(3):
-            cross_own[way, s] = out_ref[s, pl.ds(kept + way * cap, cap), :] * live
+            cross_own[way, s] = out_ref[s, 0, :, pl.ds(P_KEEP + way * CAP, CAP)] * live
         crossing.append(remote(cross_own.at[way], cross_in.at[way], 7 + way, at(1 - 2 * way, 0)))
         crossing[-1].start()
     lax.fori_loop(0, kept, one, 0)
     for way in range(2):
         crossing[way].wait()
         for s in range(3):
-            out_ref[s, pl.ds(kept + way * cap, cap), :] = cross_in[way, s]
+            out_ref[s, 0, :, pl.ds(P_KEEP + way * CAP, CAP)] = cross_in[way, s]
     for copy in far:
         copy.wait()
 
@@ -244,16 +250,12 @@
     n_fields, levels, width_x, width_y = fields.shape
     columns = n_fields * levels
     packed = (columns * GROUP // LANES * width_x, LANES)
-    blocks = cells.shape[0] // LANES
-    half = LANES // 2
-    column = cells % width_y
-    tile = cells // width_y + 1 + jnp.where(column == width_y - 1, levels * width_x, 0)
-    pairs = column.reshape(-1, half)
-    pairs = jnp.concatenate([pairs, (pairs + 1) % width_y], axis=1)
+    blocks = cells.shape[2] // LANES
+    tile = cells // width_y + 1 + jnp.where(cells % width_y == width_y - 1, levels * width_x, 0)
     f32 = jnp.float32
     vmem = pl.BlockSpec(memory_space=pltpu.VMEM)
     smem = pl.BlockSpec(memory_space=pltpu.SMEM)
-    shapes = [(2, columns, LANES), (2, columns, LANES), packed, (8, LANES), (3, blocks, LANES)]
+    shapes = [(2, columns, LANES), (2, columns, LANES), packed, (8, LANES), offsets.shape]
     return pl.pallas_call(
         functools.partial(advance_kernel, n_gx, n_gy, n_fields, levels, width_x, blocks),
         out_shape=[jax.ShapeDtypeStruct(s, f32) for s in shapes],
@@ -271,8 +273,8 @@
             pltpu.VMEM((8, LANES), f32),
             pltpu.VMEM((n_gy, 8, LANES), f32),
             pltpu.VMEM((n_gx, 8, LANES), f32),
-            pltpu.VMEM((2, 3, CAP // LANES, LANES), f32),
-            pltpu.VMEM((2, 3, CAP // LANES, LANES), f32),
+            pltpu.VMEM((2, 3, 1, CAP), f32),
+            pltpu.VMEM((2, 3, 1, CAP), f32),
             pltpu.SemaphoreType.DMA,
             pltpu.SemaphoreType.DMA((9,)),
             pltpu.SemaphoreType.DMA((9,)),
@@ -284,15 +286,14 @@
         compiler_params=pltpu.CompilerParams(
             collective_id=0, has_side_effects=True, vmem_limit_bytes=VMEM_BYTES
         ),
-    )(tile, counts, pairs, offsets.reshape(3, blocks, LANES), fields.reshape(-1, width_y))
+    )(tile, counts, cells, offsets, fields.reshape(-1, width_y))
 
 
 def stencil_kernel(
     levels, width_x, x_ref, vel_ref, prior_ref, heights_ref, low_ref, high_ref, cols_ref, speed_ref,
-    new_ref, acc_ref, ext,
+    new_ref, acc_ref, ext, band,
 ):
     span = width_x + 16
-    per_pack = LANES // GROUP
     step = section_weight * (courant / (speed_ref[0:1, :] + 1e-06))
     zero = jnp.zeros((span, LANES), jnp.float32)
     ext[0:span, :] = zero
@@ -307,43 +308,59 @@
     for d in range(2):
         ext[pl.ds(span + 6 + d, levels, stride=span), :] = low_ref[d]
         ext[pl.ds(span + 8 + width_x + d, levels, stride=span), :] = high_ref[d]
-    lanes = lane_ids(width_x)
     heights = heights_ref[...]
 
-    def level(half, i):
-        k = half * per_pack + i
-        base = pl.multiple_of((k + 1) * span, 8)
-        center = ext[pl.ds(base + 8, width_x), :]
-
-        def along(d):
-            return ext[pl.ds(base + 8 + d, width_x), :]
-
-        up = ext[pl.ds(base + span + 8, width_x), :]
-        down = ext[pl.ds(base - span + 8, width_x), :]
-        edge = pltpu.roll(cols_ref[0, half], unpack_shift(i), 1)
-        right1 = pltpu.roll(jnp.where(lanes == 0, edge, center), LANES - 1, 1)
-        right2 = pltpu.roll(jnp.where(lanes <= 1, edge, center), LANES - 2, 1)
-        left1 = pltpu.roll(jnp.where(lanes == LANES - 1, edge, center), 1, 1)
-        left2 = pltpu.roll(jnp.where(lanes >= LANES - 2, edge, center), 2, 1)
-        low1, high1 = along(-1), along(1)
-        grad_x = (high1 - low1) * (8.0 / 12.0) - (along(2) - along(-2)) * (1.0 / 12.0)
-        grad_y = (right1 - left1) * (8.0 / 12.0) - (right2 - left2) * (1.0 / 12.0)
-        grad_z = 0.5 * (up - down)
-        laplace = high1 + low1 + right1 + left1 + up + down - 6.0 * center
-        tendency = viscosity * laplace - (
-            vel_ref[0, k] * grad_x + vel_ref[1, k] * grad_y + vel_ref[2, k] * grad_z
-        )
-        acc = prior_weight * prior_ref[0, k] + tendency
-        fluid = k >= heights
-        acc_ref[0, k] = jnp.where(fluid, acc, 0.0)
-        new_ref[0, k] = jnp.where(fluid, center + step * acc, 0.0)
-
-    def some(half, carry):
-        for i in range(per_pack):
-            level(half, i)
-        return carry
-
-    lax.fori_loop(0, levels // per_pack, some, 0)
+    @pl.when(pl.program_id(0) == 0)
+    def _():
+        source = lax.broadcasted_iota(jnp.int32, (2 * LANES, 2 * LANES), 0)
+        target = lax.broadcasted_iota(jnp.int32, (2 * LANES, 2 * LANES), 1)
+        edge = source - LANES
+        outer = jnp.where(edge <= 1, source, jnp.where(edge >= LANES - 2, edge - LANES, 4 * LANES))
+        place = jnp.where(source < LANES, source, outer)
+        apart = place - jnp.where(target < LANES, target, target - LANES)
+        size = jnp.abs(apart)
+        slope = jnp.where(size == 1, 8 * apart, jnp.where(size == 2, -apart // 2, 0))
+        total = jnp.where(size == 1, 1, 0)
+        band[...] = jnp.where(target < LANES, slope, total).astype(jnp.float32).astype(jnp.bfloat16)
+
+    unroll = 4
+
+    def some(n, edges):
+        first = n * unroll
+        centers = [ext[pl.ds(pl.multiple_of((first + i + 1) * span + 8, 8), width_x), :] for i in range(unroll)]
+        sides = [pltpu.roll(edges, unpack_shift(i), 1) for i in range(unroll)]
+        both = jnp.concatenate(
+            [jnp.concatenate(centers, axis=0), jnp.concatenate(sides, axis=0)], axis=1
+        )
+        coarse = both.astype(jnp.bfloat16)
+        fine = (both - coarse.astype(jnp.float32)).astype(jnp.bfloat16)
+        across = jnp.dot(coarse, band[...], preferred_element_type=jnp.float32)
+        across += jnp.dot(fine, band[...], preferred_element_type=jnp.float32)
+        for i in range(unroll):
+            k = first + i
+            base = pl.multiple_of((k + 1) * span, 8)
+            center = centers[i]
+            mine = across[i * width_x : (i + 1) * width_x]
+
+            def along(d):
+                return ext[pl.ds(base + 8 + d, width_x), :]
+
+            up = ext[pl.ds(base + span + 8, width_x), :]
+            down = ext[pl.ds(base - span + 8, width_x), :]
+            low1, high1 = along(-1), along(1)
+            grad_x = (high1 - low1) * 8.0 - (along(2) - along(-2))
+            turn = vel_ref[0, k] * grad_x + vel_ref[1, k] * mine[:, :LANES]
+            laplace = high1 + low1 + mine[:, LANES:] + up + down - 6.0 * center
+            tendency = viscosity * laplace - (turn * (1.0 / 12.0) + vel_ref[2, k] * (0.5 * (up - down)))
+            acc = prior_weight * prior_ref[0, k] + tendency
+            fluid = k >= heights
+            acc_ref[0, k] = jnp.where(fluid, acc, 0.0)
+            new_ref[0, k] = jnp.where(fluid, center + step * acc, 0.0)
+        return pltpu.roll(edges, LANES - GROUP * unroll, 1)
+
+    steps = LANES // GROUP // unroll
+    for half in range(levels // (steps * unroll)):
+        lax.fori_loop(half * steps, (half + 1) * steps, some, cols_ref[0, half])
 
 
 def stencil(fields, previous, heights, low, high, cols, speed):
@@ -365,17 +382,20 @@
             pl.BlockSpec((8, LANES), lambda f: (0, 0)),
         ],
         out_specs=[block, block],
-        scratch_shapes=[pltpu.VMEM(((levels + 2) * (width_x + 16), LANES), jnp.float32)],
+        scratch_shapes=[
+            pltpu.VMEM(((levels + 2) * (width_x + 16), LANES), jnp.float32),
+            pltpu.VMEM((2 * LANES, 2 * LANES), jnp.bfloat16),
+        ],
         compiler_params=pltpu.CompilerParams(vmem_limit_bytes=VMEM_BYTES),
     )(fields, fields, previous, heights, low, high, cols.reshape(n_fields, halves, width_x, LANES), speed)
 
 
 def local(mesh, fields, previous, heights, part_cells, part_offsets, cross_counts):
     low, high, cols, speed, moved = advance(
-        mesh, fields, part_cells[0, 0], part_offsets[:, 0, 0], cross_counts[0, 0]
+        mesh, fields, part_cells, part_offsets, cross_counts
     )
     updated, accumulated = stencil(fields, previous, heights, low, high, cols, speed)
-    return (updated, accumulated, moved.reshape(3, 1, 1, -1))
+    return (updated, accumulated, moved)
 
 
 def solution(mesh):

time: 72.4 us -> 71.4 us (0.986)
  the two profiles are of different devices: /device:TPU:0 before, /device:TPU:27 now
where the time goes in v3:
time: 71.4 us; the launch traced here: 71.1 us
  Pallas kernels  68.1 us (95%)
  other arithmetic  1.67 us (2%)
    pallas_call x1, Pallas kernels, advance(): pl.pallas_call(functools.partial(advance_kernel, n_gx, n_gy, n_fields, le...  45.6 us
    pallas_call x1, Pallas kernels, stencil(): pl.pallas_call(functools.partial(stencil_kernel, levels, width_x), grid=(...  22.6 us
    add x1, other arithmetic, advance(): cells // width_y + 1  1.67 us

profile of v3, /device:TPU:27, one launch (start us, length us, event | category | flops | bytes accessed | tf_op | source)
XLA Modules:
  0.0 71.1 jit_solution(4193188141931922841)
XLA Ops:
  0.6 1.7 %fusion.tile_ref = s32[1,1,9216]{2,1,0:T(1,128)} fusion(s32[1,1,9216]{2,1,0:T(1,128)} %cell_ref.1), kind=kLoop, calls=%fused_computation.6 | loop fusion | flops 211968 | bytes 73728 | tf_op jit(solution)/shard_map/add | solution.py:254
  2.3 45.6 %shard_map.85 = (f32[2,320,128]{2,1,0:T(8,128)}, f32[2,320,128]{2,1,0:T(8,128)}, f32[160,128]{1,0:T(8,128)}, f32[8,128]{1,0:T(8,128)}, f32[3,1,1,9216]{3,2,1,0:T(1,128)}) custom-call(s32[1,1,9216]{2,1,0:T(1,128)} %fusion.tile_ref, s32[1,1,2]{2,1,0:T(1,128)} %counts_ref.1, s32[1,1,9216]{2,1,0:T(1,128)} %cell_ref.1, f32[3,1,1,9216]{3,2,1,0:T(1,128)} %off_ref.1, ...), custom_call_target="tpu_custom_call" | custom-call | tf_op jit(solution)/shard_map/pallas_call | solution.py:259
  47.9 0.0 copy-start
  47.9 22.6 %shard_map.86 = (f32[5,64,16,128]{3,2,1,0:T(8,128)}, f32[5,64,16,128]{3,2,1,0:T(8,128)}) custom-call(f32[5,64,16,128]{3,2,1,0:T(8,128)} %vel_ref.1, f32[5,64,16,128]{3,2,1,0:T(8,128)} %vel_ref.1, f32[5,64,16,128]{3,2,1,0:T(8,128)} %prior_ref.1, s32[16,128]{1,0:T(8,128)} %heights_ref.1, f32[2,320,128]{2,1,0:T(8,128)} %get-tuple-element.10.low_ref, ...), custom_call_target="tpu_custom_call" | custom-call | tf_op jit(solution)/shard_map/pallas_call | solution.py:370
  70.5 0.0 copy-done
  70.5 0.6 copy.10
Async XLA Ops:
  47.9 22.6 %copy-start = (f32[3,1,1,9216]{3,2,1,0:T(1,128)S(1)}, f32[3,1,1,9216]{3,2,1,0:T(1,128)}, u32[]{:S(2)}) copy-start(f32[3,1,1,9216]{3,2,1,0:T(1,128)} %get-tuple-element.22) | copy-start | bytes 331780

commit v4 on v3

--- a/solution.py
+++ b/solution.py
@@ -213,7 +213,7 @@
             ids = jnp.broadcast_to(ids, (8, LANES))
             got = jnp.zeros((8, LANES), jnp.float32)
             for i in range(half):
-                tile = table[tile_ref[0, 0, j * LANES + h * half + i]]
+                tile = table[tile_ref[j, h * half + i]]
                 turned = jnp.take_along_axis(tile, ids, axis=1, mode="promise_in_bounds")
                 got = jnp.where(place == i, turned, got)
             got = got * weight
@@ -286,12 +286,12 @@
         compiler_params=pltpu.CompilerParams(
             collective_id=0, has_side_effects=True, vmem_limit_bytes=VMEM_BYTES
         ),
-    )(tile, counts, cells, offsets, fields.reshape(-1, width_y))
+    )(tile.reshape(blocks, LANES), counts, cells, offsets, fields.reshape(-1, width_y))
 
 
 def stencil_kernel(
     levels, width_x, x_ref, vel_ref, prior_ref, heights_ref, low_ref, high_ref, cols_ref, speed_ref,
-    new_ref, acc_ref, ext, band,
+    new_ref, acc_ref, ext, band, halves, across,
 ):
     span = width_x + 16
     step = section_weight * (courant / (speed_ref[0:1, :] + 1e-06))
@@ -324,43 +324,54 @@
         band[...] = jnp.where(target < LANES, slope, total).astype(jnp.float32).astype(jnp.bfloat16)
 
     unroll = 4
-
-    def some(n, edges):
+    rows = levels * width_x
+
+    def split(n, edges):
+        for i in range(unroll):
+            k = n * unroll + i
+            side = pltpu.roll(edges, unpack_shift(i), 1)
+            for part, value in enumerate((x_ref[0, k], side)):
+                coarse = value.astype(jnp.bfloat16)
+                fine = (value - coarse.astype(jnp.float32)).astype(jnp.bfloat16)
+                here = pl.ds(part * LANES, LANES)
+                halves[pl.ds(pl.multiple_of(k * width_x, width_x), width_x), here] = coarse
+                halves[pl.ds(pl.multiple_of(rows + k * width_x, width_x), width_x), here] = fine
+        return pltpu.roll(edges, LANES - GROUP * unroll, 1)
+
+    steps = LANES // GROUP // unroll
+    for half in range(levels // (steps * unroll)):
+        lax.fori_loop(half * steps, (half + 1) * steps, split, cols_ref[0, half])
+    across[...] = jnp.dot(halves[0:rows], band[...], preferred_element_type=jnp.float32) + jnp.dot(
+        halves[rows:], band[...], preferred_element_type=jnp.float32
+    )
+
+    def some(n, carry):
         first = n * unroll
-        centers = [ext[pl.ds(pl.multiple_of((first + i + 1) * span + 8, 8), width_x), :] for i in range(unroll)]
-        sides = [pltpu.roll(edges, unpack_shift(i), 1) for i in range(unroll)]
-        both = jnp.concatenate(
-            [jnp.concatenate(centers, axis=0), jnp.concatenate(sides, axis=0)], axis=1
-        )
-        coarse = both.astype(jnp.bfloat16)
-        fine = (both - coarse.astype(jnp.float32)).astype(jnp.bfloat16)
-        across = jnp.dot(coarse, band[...], preferred_element_type=jnp.float32)
-        across += jnp.dot(fine, band[...], preferred_element_type=jnp.float32)
         for i in range(unroll):
+            mine = pl.ds(pl.multiple_of((first + i) * width_x, width_x), width_x)
+            slope = across[mine, 0:LANES]
+            beside = across[mine, LANES : 2 * LANES]
             k = first + i
             base = pl.multiple_of((k + 1) * span, 8)
-            center = centers[i]
-            mine = across[i * width_x : (i + 1) * width_x]
 
             def along(d):
                 return ext[pl.ds(base + 8 + d, width_x), :]
 
+            center = along(0)
             up = ext[pl.ds(base + span + 8, width_x), :]
             down = ext[pl.ds(base - span + 8, width_x), :]
             low1, high1 = along(-1), along(1)
             grad_x = (high1 - low1) * 8.0 - (along(2) - along(-2))
-            turn = vel_ref[0, k] * grad_x + vel_ref[1, k] * mine[:, :LANES]
-            laplace = high1 + low1 + mine[:, LANES:] + up + down - 6.0 * center
+            turn = vel_ref[0, k] * grad_x + vel_ref[1, k] * slope
+            laplace = high1 + low1 + beside + up + down - 6.0 * center
             tendency = viscosity * laplace - (turn * (1.0 / 12.0) + vel_ref[2, k] * (0.5 * (up - down)))
             acc = prior_weight * prior_ref[0, k] + tendency
             fluid = k >= heights
             acc_ref[0, k] = jnp.where(fluid, acc, 0.0)
             new_ref[0, k] = jnp.where(fluid, center + step * acc, 0.0)
-        return pltpu.roll(edges, LANES - GROUP * unroll, 1)
-
-    steps = LANES // GROUP // unroll
-    for half in range(levels // (steps * unroll)):
-        lax.fori_loop(half * steps, (half + 1) * steps, some, cols_ref[0, half])
+        return carry
+
+    lax.fori_loop(0, levels // unroll, some, 0)
 
 
 def stencil(fields, previous, heights, low, high, cols, speed):
@@ -385,6 +396,8 @@
         scratch_shapes=[
             pltpu.VMEM(((levels + 2) * (width_x + 16), LANES), jnp.float32),
             pltpu.VMEM((2 * LANES, 2 * LANES), jnp.bfloat16),
+            pltpu.VMEM((2 * levels * width_x, 2 * LANES), jnp.bfloat16),
+            pltpu.VMEM((levels * width_x, 2 * LANES), jnp.float32),
         ],
         compiler_params=pltpu.CompilerParams(vmem_limit_bytes=VMEM_BYTES),
     )(fields, fields, previous, heights, low, high, cols.reshape(n_fields, halves, width_x, LANES), speed)

time: 71.4 us -> 64.8 us (0.908)
  Pallas kernels: 68.1 us -> 61.6 us
    pallas_call x1, Pallas kernels: 22.6 us -> 16 us  [stencil(): pl.pallas_call(functools.partial(stencil_kernel, levels, width_x), grid=(...]
where the time goes in v4:
time: 64.8 us; the launch traced here: 64.6 us
  Pallas kernels  61.6 us (95%)
  other arithmetic  1.67 us (3%)
  local copies, waits for them, and re-layouts  0.65 us (1%)
  between operations  0.65 us (1%)
    pallas_call x1, Pallas kernels, advance(): pl.pallas_call(functools.partial(advance_kernel, n_gx, n_gy, n_fields, le...  45.6 us
    pallas_call x1, Pallas kernels, stencil(): pl.pallas_call(functools.partial(stencil_kernel, levels, width_x), grid=(...  16 us
    add x1, other arithmetic, advance(): cells // width_y + 1  1.67 us

profile of v4, /device:TPU:27, one launch (start us, length us, event | category | flops | bytes accessed | tf_op | source)
XLA Modules:
  0.0 64.6 jit_solution(5754967305732671977)
XLA Ops:
  0.6 1.7 %fusion = s32[1,1,9216]{2,1,0:T(1,128)} fusion(s32[1,1,9216]{2,1,0:T(1,128)} %cell_ref.1), kind=kLoop, calls=%fused_computation.6 | loop fusion | flops 211968 | bytes 73728 | tf_op jit(solution)/shard_map/add | solution.py:254
  2.3 45.6 %shard_map.85 = (f32[2,320,128]{2,1,0:T(8,128)}, f32[2,320,128]{2,1,0:T(8,128)}, f32[160,128]{1,0:T(8,128)}, f32[8,128]{1,0:T(8,128)}, f32[3,1,1,9216]{3,2,1,0:T(1,128)}) custom-call(s32[72,128]{1,0:T(8,128)} %bitcast.4, s32[1,1,2]{2,1,0:T(1,128)} %counts_ref.1, s32[1,1,9216]{2,1,0:T(1,128)} %cell_ref.1, f32[3,1,1,9216]{3,2,1,0:T(1,128)} %off_ref.1, ...), custom_call_target="tpu_custom_call" | custom-call | tf_op jit(solution)/shard_map/pallas_call | solution.py:259
  47.9 0.0 copy-start
  47.9 16.0 %shard_map.86 = (f32[5,64,16,128]{3,2,1,0:T(8,128)}, f32[5,64,16,128]{3,2,1,0:T(8,128)}) custom-call(f32[5,64,16,128]{3,2,1,0:T(8,128)} %vel_ref.1, f32[5,64,16,128]{3,2,1,0:T(8,128)} %vel_ref.1, f32[5,64,16,128]{3,2,1,0:T(8,128)} %prior_ref.1, s32[16,128]{1,0:T(8,128)} %heights_ref.1, f32[2,320,128]{2,1,0:T(8,128)} %get-tuple-element.10.low_ref, ...), custom_call_target="tpu_custom_call" | custom-call | tf_op jit(solution)/shard_map/pallas_call | solution.py:381
  63.9 0.0 copy-done
  63.9 0.6 %copy.10 = f32[3,1,1,9216]{3,2,1,0:T(1,128)} copy(f32[3,1,1,9216]{3,2,1,0:T(1,128)S(1)} %copy-done) | data formatting | bytes 221184
Async XLA Ops:
  47.9 16.1 %copy-start = (f32[3,1,1,9216]{3,2,1,0:T(1,128)S(1)}, f32[3,1,1,9216]{3,2,1,0:T(1,128)}, u32[]{:S(2)}) copy-start(f32[3,1,1,9216]{3,2,1,0:T(1,128)} %get-tuple-element.22) | copy-start | bytes 331780

commit v5 on v4

--- a/solution.py
+++ b/solution.py
@@ -1,4 +1,5 @@
 import functools
+import math
 
 import jax
 import jax.numpy as jnp
@@ -34,7 +35,7 @@
     tile_ref, counts_ref, cell_ref, off_ref, x_hbm,
     low_ref, high_ref, cols_ref, speed_ref, out_ref,
     x_ref, table, planes, corner_ref, packed, from_left, from_right, speed_own, speed_row, speed_y, speed_x,
-    cross_own, cross_in,
+    cross_own, cross_in, ids_rows, got_rows,
     load_sem, send_sems, recv_sems, y_send, y_recv, x_send, x_recv,
 ):
     p = lax.axis_index("gx")
@@ -147,6 +148,17 @@
         return carry
 
     lax.fori_loop(0, levels, build_own, 0, unroll=2)
+    turn = LANES // 2
+    early_lane = lane_ids(1) < turn
+
+    def columns_of(j, carry):
+        column = cell_ref[0, :, pl.ds(pl.multiple_of(j * LANES, LANES), LANES)] % LANES
+        other = pltpu.roll(column, turn, 1)
+        ids_rows[pl.ds(2 * j, 1), :] = jnp.where(early_lane, column, (other + 1) % LANES)
+        ids_rows[pl.ds(2 * j + 1, 1), :] = jnp.where(early_lane, other, (column + 1) % LANES)
+        return carry
+
+    lax.fori_loop(0, blocks, columns_of, 0, unroll=4)
 
     for copy in side:
         copy.wait()
@@ -195,39 +207,41 @@
     sub = lax.broadcasted_iota(jnp.int32, (8, LANES), 0)
     place = lanes % half
 
-    def one(j, carry):
-        sums = []
-        here = pl.ds(pl.multiple_of(j * LANES, LANES), LANES)
-        column = cell_ref[0, :, here] % LANES
-        column_other = pltpu.roll(column, half, 1)
-        frac = off_ref[1, 0, :, here]
-        other = pltpu.roll(frac, half, 1)
-        early = lanes[0:1] < half
+    def gather(j, carry):
         for h in range(2):
-            if h == 0:
-                ids = jnp.where(early, column, (column_other + 1) % LANES)
-                weight = jnp.where(early, 1.0 - frac, other)
-            else:
-                ids = jnp.where(early, column_other, (column + 1) % LANES)
-                weight = jnp.where(early, 1.0 - other, frac)
-            ids = jnp.broadcast_to(ids, (8, LANES))
+            ids = jnp.broadcast_to(ids_rows[pl.ds(2 * j + h, 1), :], (8, LANES))
             got = jnp.zeros((8, LANES), jnp.float32)
             for i in range(half):
                 tile = table[tile_ref[j, h * half + i]]
                 turned = jnp.take_along_axis(tile, ids, axis=1, mode="promise_in_bounds")
                 got = jnp.where(place == i, turned, got)
-            got = got * weight
-            sums.append(got + pltpu.roll(got, half, 1))
-        both = jnp.where(lanes < half, sums[0], sums[1])
+            got_rows[2 * j + h] = got
+        return carry
+
+    def finish(j):
+        here = pl.ds(pl.multiple_of(j * LANES, LANES), LANES)
+        frac = off_ref[1, 0, :, here]
+        other = pltpu.roll(frac, half, 1)
+        early = lanes[0:1] < half
+        first = got_rows[2 * j] * jnp.where(early, 1.0 - frac, other)
+        second = got_rows[2 * j + 1] * jnp.where(early, 1.0 - other, frac)
+        both = jnp.where(lanes < half, first + pltpu.roll(first, half, 1), second + pltpu.roll(second, half, 1))
         frac = off_ref[0, 0, :, here]
         both = both * jnp.where(sub < 3, 1.0 - frac, frac)
         vel = both[0:3] + both[3:6]
         for s in range(3):
             out_ref[s, 0, :, here] = off_ref[s, 0, :, here] + time_step * vel[s : s + 1]
+
+    group = math.gcd(math.gcd(P_KEEP // LANES, 2 * CAP // LANES), 4)
+
+    def finish_some(n, carry):
+        for i in range(group):
+            finish(n * group + i)
         return carry
 
     kept = P_KEEP // LANES
-    lax.fori_loop(kept, blocks, one, 0)
+    lax.fori_loop(kept, blocks, gather, 0)
+    lax.fori_loop(kept // group, blocks // group, finish_some, 0)
     slots = lax.broadcasted_iota(jnp.int32, (1, CAP), 1)
     crossing = []
     for way in range(2):
@@ -236,7 +250,8 @@
             cross_own[way, s] = out_ref[s, 0, :, pl.ds(P_KEEP + way * CAP, CAP)] * live
         crossing.append(remote(cross_own.at[way], cross_in.at[way], 7 + way, at(1 - 2 * way, 0)))
         crossing[-1].start()
-    lax.fori_loop(0, kept, one, 0)
+    lax.fori_loop(0, kept, gather, 0)
+    lax.fori_loop(0, kept // group, finish_some, 0)
     for way in range(2):
         crossing[way].wait()
         for s in range(3):
@@ -275,6 +290,8 @@
             pltpu.VMEM((n_gx, 8, LANES), f32),
             pltpu.VMEM((2, 3, 1, CAP), f32),
             pltpu.VMEM((2, 3, 1, CAP), f32),
+            pltpu.VMEM((2 * blocks, LANES), jnp.int32),
+            pltpu.VMEM((2 * blocks, 8, LANES), f32),
             pltpu.SemaphoreType.DMA,
             pltpu.SemaphoreType.DMA((9,)),
             pltpu.SemaphoreType.DMA((9,)),

time: 64.8 us -> 56.3 us (0.87)
  Pallas kernels: 61.6 us -> 53 us
    pallas_call x1, Pallas kernels: 45.6 us -> 37 us  [advance(): pl.pallas_call(functools.partial(advance_kernel, n_gx, n_gy, n_fields, le...]
where the time goes in v5:
time: 56.3 us; the launch traced here: 56 us
  Pallas kernels  53 us (94%)
  other arithmetic  1.67 us (3%)
  local copies, waits for them, and re-layouts  0.65 us (1%)
  between operations  0.65 us (1%)
    pallas_call x1, Pallas kernels, advance(): pl.pallas_call(functools.partial(advance_kernel, n_gx, n_gy, n_fields, le...  37 us
    pallas_call x1, Pallas kernels, stencil(): pl.pallas_call(functools.partial(stencil_kernel, levels, width_x), grid=(...  16 us
    add x1, other arithmetic, advance(): cells // width_y + 1  1.67 us

profile of v5, /device:TPU:27, one launch (start us, length us, event | category | flops | bytes accessed | tf_op | source)
XLA Modules:
  0.0 56.0 jit_solution(18127753418072608322)
XLA Ops:
  0.6 1.7 %fusion = s32[1,1,9216]{2,1,0:T(1,128)} fusion(s32[1,1,9216]{2,1,0:T(1,128)} %cell_ref.1), kind=kLoop, calls=%fused_computation.6 | loop fusion | flops 211968 | bytes 73728 | tf_op jit(solution)/shard_map/add | solution.py:269
  2.3 37.0 %shard_map.85 = (f32[2,320,128]{2,1,0:T(8,128)}, f32[2,320,128]{2,1,0:T(8,128)}, f32[160,128]{1,0:T(8,128)}, f32[8,128]{1,0:T(8,128)}, f32[3,1,1,9216]{3,2,1,0:T(1,128)}) custom-call(s32[72,128]{1,0:T(8,128)} %bitcast.4, s32[1,1,2]{2,1,0:T(1,128)} %counts_ref.1, s32[1,1,9216]{2,1,0:T(1,128)} %cell_ref.1, f32[3,1,1,9216]{3,2,1,0:T(1,128)} %off_ref.1, ...), custom_call_target="tpu_custom_call" | custom-call | tf_op jit(solution)/shard_map/pallas_call | solution.py:274
  39.3 0.0 copy-start
  39.3 16.0 %shard_map.86 = (f32[5,64,16,128]{3,2,1,0:T(8,128)}, f32[5,64,16,128]{3,2,1,0:T(8,128)}) custom-call(f32[5,64,16,128]{3,2,1,0:T(8,128)} %vel_ref.1, f32[5,64,16,128]{3,2,1,0:T(8,128)} %vel_ref.1, f32[5,64,16,128]{3,2,1,0:T(8,128)} %prior_ref.1, s32[16,128]{1,0:T(8,128)} %heights_ref.1, f32[2,320,128]{2,1,0:T(8,128)} %get-tuple-element.10.low_ref, ...), custom_call_target="tpu_custom_call" | custom-call | tf_op jit(solution)/shard_map/pallas_call | solution.py:398
  55.3 0.0 copy-done
  55.4 0.6 %copy.10 = f32[3,1,1,9216]{3,2,1,0:T(1,128)} copy(f32[3,1,1,9216]{3,2,1,0:T(1,128)S(1)} %copy-done) | data formatting | bytes 221184
Async XLA Ops:
  39.3 16.0 %copy-start = (f32[3,1,1,9216]{3,2,1,0:T(1,128)S(1)}, f32[3,1,1,9216]{3,2,1,0:T(1,128)}, u32[]{:S(2)}) copy-start(f32[3,1,1,9216]{3,2,1,0:T(1,128)} %get-tuple-element.22) | copy-start | bytes 331780
